TPU v7x, 256 devices: a whole 4x4x8 slice. The times are simulated.
256 devices in a mesh: dp: 8 (over y, core), cuts: 32 (over x, z).
Axes of the slice: x: 4, y: 4, z: 8, core: 2. Of those that a mesh axis runs over, the one named last changes fastest.
Arguments:
- activations: bfloat16 [32768, 4096], P(('dp', 'cuts')), parts along dimension 0, may hold values from -6 to 6
- output_gradients: bfloat16 [32768, 14336], P(('dp', 'cuts')), parts along dimension 0, may hold values from -6 to 6
- adapter_down: bfloat16 [4096, 16], replicated, may hold values from -0.09375 to 0.09375
- adapter_up: bfloat16 [16, 14336], replicated, may hold values from -0.046875 to 0.046875
- token_example_number: int32 [32768], P(('dp', 'cuts')), parts along dimension 0, may hold values from 0 to 63, as said below
- cut_first_example: int32 [264], P('dp'), parts along dimension 0, may hold values from 0 to 64, as said below
- block_seeds: int32 [32], replicated, may hold values from 0 to 1073741823
Outputs:
- features: float32 [512, 4096], P(('dp', 'cuts')), parts along dimension 0
There are 8 independent parts, one for each index of `dp`. A program takes and returns all parts, laid end to end along the dimension named above; an argument that names none is the same for every part. Nothing has to cross between parts.
Inputs may be any that keep to these rules, and one draw needn't show every extreme that they name: `token_example_number`: within the 128 rows of each index d of cuts the example numbers never fall and take every value from cut_first_example[d] to cut_first_example[d+1] - 1; no example spans two indices. `cut_first_example`: starts at 0, ends at 64; each index of cuts holds 1 to 4 examples and some index holds exactly 4.
All inputs are finite; a program needn't handle non-finite values.
Results may differ from a plain program's by a relative error of at most 0.0041.
Values may be sent and summed in bfloat16 or wider, within the bound.
No kernel may reach another device: no remote copies, remote signals or barrier semaphores. Data moves between devices by JAX's collectives and lax.ppermute only.
A program may use at most 128 MiB of HBM per device.

v0:
```python
import jax
import jax.numpy as jnp
from jax import lax
from jax.sharding import PartitionSpec as P

MODEL_WIDTH = 4096
HIDDEN_UNITS = 14336
ADAPTER_RANK = 16
SKETCH = 4096
PANEL = 256
EXMAX = 4
EX_AVG = 2


def rademacher(seed_value, first_row, row_count, col_count):
    feature_ids = (first_row + lax.iota(jnp.int32, row_count))[:, None]
    param_ids = lax.iota(jnp.int32, col_count)[None, :]
    mixed = param_ids * 1640531527 + feature_ids * 668265263 + seed_value
    mixed = mixed ^ jnp.right_shift(mixed, 15) & 131071
    mixed = mixed * 739982445
    mixed = mixed ^ jnp.right_shift(mixed, 13) & 524287
    picked = jnp.right_shift(mixed, 20) & 1
    return (2 * picked - 1).astype(jnp.bfloat16)


def example_rows(cut_first_example, owners, slot_cap, example_total):
    example_ids = lax.iota(jnp.int32, example_total)
    holder = jnp.sum(
        (cut_first_example[None, 1 : owners + 1] <= example_ids[:, None]).astype(jnp.int32), axis=1
    )
    start_ids = jnp.take(cut_first_example, holder)
    return holder * slot_cap + example_ids - start_ids


def sketch_rows(rows_a, rows_b, block_seeds, owner, per_owner):
    row_total = rows_a.shape[0]
    a_width = rows_a.shape[2] // per_owner
    b_width = rows_b.shape[2] // per_owner
    block_len = ADAPTER_RANK * (a_width + b_width)
    part_a = rows_a.reshape(row_total, ADAPTER_RANK * a_width)
    part_b = rows_b.reshape(row_total, ADAPTER_RANK * b_width)
    vector = jnp.concatenate([part_a, part_b], axis=1)
    seed_value = block_seeds[owner * per_owner + 0]

    def one_panel(panel_idx):
        signs = rademacher(seed_value, panel_idx * PANEL, PANEL, block_len)
        return lax.dot_general(
            vector, signs, (((1,), (1,)), ((), ())), preferred_element_type=jnp.float32
        )

    pieces = lax.map(one_panel, jnp.arange(SKETCH // PANEL, dtype=jnp.int32))
    total = jnp.moveaxis(pieces, 0, 1).reshape(row_total, SKETCH)
    return total


def body(
    activations,
    output_gradients,
    adapter_down,
    adapter_up,
    token_example_number,
    cut_first_example,
    block_seeds,
):
    owners = lax.axis_size("cuts")
    owner = lax.axis_index("cuts")
    tok_count = activations.shape[0]
    per_owner = block_seeds.shape[0] // owners
    up_matrix = lax.dot_general(
        output_gradients, adapter_up, (((1,), (1,)), ((), ())), preferred_element_type=jnp.float32
    ).astype(jnp.bfloat16)
    down_matrix = jnp.dot(activations, adapter_down, preferred_element_type=jnp.float32).astype(
        jnp.bfloat16
    )
    slot_ids = token_example_number - cut_first_example[owner]
    onehot = (slot_ids[:, None] == lax.iota(jnp.int32, EXMAX)[None, :]).astype(jnp.bfloat16)
    spread_up = (up_matrix[:, None, :] * onehot[:, :, None]).reshape(
        tok_count, EXMAX * ADAPTER_RANK
    )
    spread_down = (down_matrix[:, None, :] * onehot[:, :, None]).reshape(
        tok_count, EXMAX * ADAPTER_RANK
    )
    grad_a = lax.dot_general(
        spread_up, activations, (((0,), (0,)), ((), ())), preferred_element_type=jnp.float32
    )
    grad_b = lax.dot_general(
        spread_down, output_gradients, (((0,), (0,)), ((), ())), preferred_element_type=jnp.float32
    )
    grad_a = grad_a.astype(jnp.bfloat16).reshape(EXMAX, ADAPTER_RANK, -1)
    grad_b = grad_b.astype(jnp.bfloat16).reshape(EXMAX, ADAPTER_RANK, -1)
    rows_a, rows_b = (
        lax.all_to_all(grad_a, "cuts", split_axis=2, concat_axis=0, tiled=True),
        lax.all_to_all(grad_b, "cuts", split_axis=2, concat_axis=0, tiled=True),
    )
    picked = example_rows(cut_first_example, owners, EXMAX, owners * EX_AVG)
    partial_value = jnp.take(
        sketch_rows(rows_a, rows_b, block_seeds, owner, per_owner), picked, axis=0
    )
    summed = lax.psum_scatter(partial_value, "cuts", scatter_dimension=0, tiled=True)
    return summed * float(ADAPTER_RANK * (MODEL_WIDTH + HIDDEN_UNITS) * tok_count) ** (-0.5)


def solution(mesh):
    in_specs = (
        P(("dp", "cuts"), None),
        P(("dp", "cuts"), None),
        P(),
        P(),
        P(("dp", "cuts")),
        P("dp"),
        P(),
    )
    out_specs = P(("dp", "cuts"), None)
    return jax.shard_map(body, mesh=mesh, in_specs=in_specs, out_specs=out_specs, check_vma=False)
```

profile of v0, /device:TPU:1, one launch (start us, length us, event | category | flops | bytes accessed | tf_op | source)
XLA Modules:
  0.0 431.5 jit_solution(254703303891505129)
XLA Ops:
  6.5 1.3 dynamic_slice.14
  7.9 1.2 broadcast_subtract_fusion
  9.1 1.3 convolution_convert_fusion.2
  10.4 3.2 convolution_convert_fusion.3
  13.9 4.6 %copy.21 = bf16[4,16,4096]{1,0,2:T(4,128)(2,1)} copy(bf16[4,16,4096]{2,1,0:T(8,128)(2,1)S(1)} %bitcast.75) | data formatting | bytes 1048576 | tf_op jit(solution)/shard_map/reshape | solution.py:89
  18.5 7.2 %reshape.154 = bf16[32,2,4096]{2,1,0:T(2,128)(2,1)} reshape(bf16[4096,4,16]{2,1,0:T(4,128)(2,1)} %bitcast.72) | data formatting | bytes 1048576
  25.7 11.9 %all-to-all-start = ((bf16[32,2,4096]{2,1,0:T(2,128)(2,1)}), bf16[32,2,4096]{2,1,0:T(2,128)(2,1)S(1)}, u32[]{:S(2)}, u32[]{:S(2)}) async-start(bf16[32,2,4096]{2,1,0:T(2,128)(2,1)} %reshape.154), calls=%async_computation | async-start | bytes 1048576 | tf_op jit(solution)/shard_map/all_to_all | solution.py:92
  37.6 2.7 convolution_convert_fusion
  40.3 14.1 %copy.23 = bf16[4,16,14336]{1,0,2:T(4,128)(2,1)} copy(bf16[4,16,14336]{2,1,0:T(8,128)(2,1)S(1)} %bitcast.74) | data formatting | bytes 3670016 | tf_op jit(solution)/shard_map/reshape | solution.py:90
  54.4 19.2 %reshape.152 = bf16[32,2,14336]{2,1,0:T(2,128)(2,1)} reshape(bf16[14336,4,16]{2,1,0:T(4,128)(2,1)} %bitcast.70) | data formatting | bytes 3670016
  73.6 9.4 %all-to-all-start.1 = ((bf16[32,2,14336]{2,1,0:T(2,128)(2,1)}), bf16[32,2,14336]{2,1,0:T(2,128)(2,1)S(1)}, u32[]{:S(2)}, u32[]{:S(2)}) async-start(bf16[32,2,14336]{2,1,0:T(2,128)(2,1)} %reshape.152), calls=%async_computation.1 | async-start | bytes 3670016 | tf_op jit(solution)/shard_map/all_to_all | solution.py:93
  83.4 0.8 gather_fusion
  84.2 0.7 dynamic_slice.13
  84.9 4.2 reshape.155
  89.1 5.3 %copy.22 = bf16[32,4,16,128]{3,2,1,0:T(8,128)(2,1)S(1)} copy(bf16[32,4,16,128]{2,1,3,0:T(4,128)(2,1)} %bitcast.73) | data formatting | bytes 1048576 | tf_op jit(solution)/shard_map/all_to_all | solution.py:92
  94.4 0.9 copy.29
  95.3 30.7 %all-to-all-done.1 = bf16[32,2,14336]{2,1,0:T(2,128)(2,1)S(1)} async-done(((bf16[32,2,14336]{2,1,0:T(2,128)(2,1)}), bf16[32,2,14336]{2,1,0:T(2,128)(2,1)S(1)}, u32[]{:S(2)}, u32[]{:S(2)}) %all-to-all-start.1) | async-done | bytes 1835040 | tf_op jit(solution)/shard_map/all_to_all | solution.py:93
  126.0 13.5 %reshape.153 = bf16[14336,4,16]{2,1,0:T(4,128)(2,1)} reshape(bf16[32,2,14336]{2,1,0:T(2,128)(2,1)S(1)} %all-to-all-done.1) | data formatting | bytes 3670016
  139.5 19.1 %copy.24 = bf16[32,4,16,448]{3,2,1,0:T(8,128)(2,1)S(1)} copy(bf16[32,4,16,448]{2,1,3,0:T(4,128)(2,1)} %bitcast.71) | data formatting | bytes 3670016 | tf_op jit(solution)/shard_map/all_to_all | solution.py:93
  158.6 3.4 reshape.133
  162.0 1.7 pad_maximum_fusion
  163.7 108.6 %while.12 = (s32[]{:T(128)}, f32[16,128,256]{1,2,0:T(8,128)}, s32[16]{0:T(128)S(1)}, s32[]{:T(128)}, bf16[128,9216]{1,0:T(8,128)(2,1)S(1)}, /*index=5*/s32[]{:T(128)}, s32[1]{0:T(128)}) while((s32[]{:T(128)}, f32[16,128,256]{1,2,0:T(8,128)}, s32[16]{0:T(128)S(1)}, s32[]{:T(128)}, bf16[128,9216]{1,0:T(8,128)(2,1)S(1)}, /*index=5*/s32[]{:T(128)}, ...), condition=%wide.region_2.3_spmd, body=%wide.region_1.2_spmd.sunk | while | flops 637019648 | bytes 2567273 | solution.py:51
  163.7 0.7 dynamic_slice.16
  165.1 5.4 %fusion.30 = f32[16,128,256]{1,2,0:T(8,128)} fusion(f32[16,128,256]{1,2,0:T(8,128)} %get-tuple-element.122, s32[]{:T(128)} %get-tuple-element.121, bf16[128,9216]{1,0:T(8,128)(2,1)S(1)} %get-tuple-element.132, s32[]{:T(128)} %get-tuple-element.131, s32[256]{0:T(256)S(1)} %add_multiply_fusion.2, s32[9216]{0:T(1024)S(1)} %iota_multiply_fusion.2), kind=kOutput, calls=%fused_computation.5.clone.1 | convolution fusion | flops 637009920 | bytes 2529280 | tf_op jit(solution)/shard_map/while/body/eval_jaxpr/dot_general | solution.py:47
  170.5 0.7 dynamic_slice.16
  171.9 5.4 %fusion.30 = f32[16,128,256]{1,2,0:T(8,128)} fusion(f32[16,128,256]{1,2,0:T(8,128)} %get-tuple-element.122, s32[]{:T(128)} %get-tuple-element.121, bf16[128,9216]{1,0:T(8,128)(2,1)S(1)} %get-tuple-element.132, s32[]{:T(128)} %get-tuple-element.131, s32[256]{0:T(256)S(1)} %add_multiply_fusion.2, s32[9216]{0:T(1024)S(1)} %iota_multiply_fusion.2), kind=kOutput, calls=%fused_computation.5.clone.1 | convolution fusion | flops 637009920 | bytes 2529280 | tf_op jit(solution)/shard_map/while/body/eval_jaxpr/dot_general | solution.py:47
  177.3 0.7 dynamic_slice.16
  178.7 5.4 %fusion.30 = f32[16,128,256]{1,2,0:T(8,128)} fusion(f32[16,128,256]{1,2,0:T(8,128)} %get-tuple-element.122, s32[]{:T(128)} %get-tuple-element.121, bf16[128,9216]{1,0:T(8,128)(2,1)S(1)} %get-tuple-element.132, s32[]{:T(128)} %get-tuple-element.131, s32[256]{0:T(256)S(1)} %add_multiply_fusion.2, s32[9216]{0:T(1024)S(1)} %iota_multiply_fusion.2), kind=kOutput, calls=%fused_computation.5.clone.1 | convolution fusion | flops 637009920 | bytes 2529280 | tf_op jit(solution)/shard_map/while/body/eval_jaxpr/dot_general | solution.py:47
  185.5 5.4 %fusion.30 = f32[16,128,256]{1,2,0:T(8,128)} fusion(f32[16,128,256]{1,2,0:T(8,128)} %get-tuple-element.122, s32[]{:T(128)} %get-tuple-element.121, bf16[128,9216]{1,0:T(8,128)(2,1)S(1)} %get-tuple-element.132, s32[]{:T(128)} %get-tuple-element.131, s32[256]{0:T(256)S(1)} %add_multiply_fusion.2, s32[9216]{0:T(1024)S(1)} %iota_multiply_fusion.2), kind=kOutput, calls=%fused_computation.5.clone.1 | convolution fusion | flops 637009920 | bytes 2529280 | tf_op jit(solution)/shard_map/while/body/eval_jaxpr/dot_general | solution.py:47
  190.9 0.7 dynamic_slice.16
  192.3 5.4 %fusion.30 = f32[16,128,256]{1,2,0:T(8,128)} fusion(f32[16,128,256]{1,2,0:T(8,128)} %get-tuple-element.122, s32[]{:T(128)} %get-tuple-element.121, bf16[128,9216]{1,0:T(8,128)(2,1)S(1)} %get-tuple-element.132, s32[]{:T(128)} %get-tuple-element.131, s32[256]{0:T(256)S(1)} %add_multiply_fusion.2, s32[9216]{0:T(1024)S(1)} %iota_multiply_fusion.2), kind=kOutput, calls=%fused_computation.5.clone.1 | convolution fusion | flops 637009920 | bytes 2529280 | tf_op jit(solution)/shard_map/while/body/eval_jaxpr/dot_general | solution.py:47
  199.1 5.4 %fusion.30 = f32[16,128,256]{1,2,0:T(8,128)} fusion(f32[16,128,256]{1,2,0:T(8,128)} %get-tuple-element.122, s32[]{:T(128)} %get-tuple-element.121, bf16[128,9216]{1,0:T(8,128)(2,1)S(1)} %get-tuple-element.132, s32[]{:T(128)} %get-tuple-element.131, s32[256]{0:T(256)S(1)} %add_multiply_fusion.2, s32[9216]{0:T(1024)S(1)} %iota_multiply_fusion.2), kind=kOutput, calls=%fused_computation.5.clone.1 | convolution fusion | flops 637009920 | bytes 2529280 | tf_op jit(solution)/shard_map/while/body/eval_jaxpr/dot_general | solution.py:47
  205.9 5.4 %fusion.30 = f32[16,128,256]{1,2,0:T(8,128)} fusion(f32[16,128,256]{1,2,0:T(8,128)} %get-tuple-element.122, s32[]{:T(128)} %get-tuple-element.121, bf16[128,9216]{1,0:T(8,128)(2,1)S(1)} %get-tuple-element.132, s32[]{:T(128)} %get-tuple-element.131, s32[256]{0:T(256)S(1)} %add_multiply_fusion.2, s32[9216]{0:T(1024)S(1)} %iota_multiply_fusion.2), kind=kOutput, calls=%fused_computation.5.clone.1 | convolution fusion | flops 637009920 | bytes 2529280 | tf_op jit(solution)/shard_map/while/body/eval_jaxpr/dot_general | solution.py:47
  211.3 0.7 dynamic_slice.16
  212.7 5.4 %fusion.30 = f32[16,128,256]{1,2,0:T(8,128)} fusion(f32[16,128,256]{1,2,0:T(8,128)} %get-tuple-element.122, s32[]{:T(128)} %get-tuple-element.121, bf16[128,9216]{1,0:T(8,128)(2,1)S(1)} %get-tuple-element.132, s32[]{:T(128)} %get-tuple-element.131, s32[256]{0:T(256)S(1)} %add_multiply_fusion.2, s32[9216]{0:T(1024)S(1)} %iota_multiply_fusion.2), kind=kOutput, calls=%fused_computation.5.clone.1 | convolution fusion | flops 637009920 | bytes 2529280 | tf_op jit(solution)/shard_map/while/body/eval_jaxpr/dot_general | solution.py:47
  219.4 5.4 %fusion.30 = f32[16,128,256]{1,2,0:T(8,128)} fusion(f32[16,128,256]{1,2,0:T(8,128)} %get-tuple-element.122, s32[]{:T(128)} %get-tuple-element.121, bf16[128,9216]{1,0:T(8,128)(2,1)S(1)} %get-tuple-element.132, s32[]{:T(128)} %get-tuple-element.131, s32[256]{0:T(256)S(1)} %add_multiply_fusion.2, s32[9216]{0:T(1024)S(1)} %iota_multiply_fusion.2), kind=kOutput, calls=%fused_computation.5.clone.1 | convolution fusion | flops 637009920 | bytes 2529280 | tf_op jit(solution)/shard_map/while/body/eval_jaxpr/dot_general | solution.py:47
  226.2 5.4 %fusion.30 = f32[16,128,256]{1,2,0:T(8,128)} fusion(f32[16,128,256]{1,2,0:T(8,128)} %get-tuple-element.122, s32[]{:T(128)} %get-tuple-element.121, bf16[128,9216]{1,0:T(8,128)(2,1)S(1)} %get-tuple-element.132, s32[]{:T(128)} %get-tuple-element.131, s32[256]{0:T(256)S(1)} %add_multiply_fusion.2, s32[9216]{0:T(1024)S(1)} %iota_multiply_fusion.2), kind=kOutput, calls=%fused_computation.5.clone.1 | convolution fusion | flops 637009920 | bytes 2529280 | tf_op jit(solution)/shard_map/while/body/eval_jaxpr/dot_general | solution.py:47
  233.0 5.4 %fusion.30 = f32[16,128,256]{1,2,0:T(8,128)} fusion(f32[16,128,256]{1,2,0:T(8,128)} %get-tuple-element.122, s32[]{:T(128)} %get-tuple-element.121, bf16[128,9216]{1,0:T(8,128)(2,1)S(1)} %get-tuple-element.132, s32[]{:T(128)} %get-tuple-element.131, s32[256]{0:T(256)S(1)} %add_multiply_fusion.2, s32[9216]{0:T(1024)S(1)} %iota_multiply_fusion.2), kind=kOutput, calls=%fused_computation.5.clone.1 | convolution fusion | flops 637009920 | bytes 2529280 | tf_op jit(solution)/shard_map/while/body/eval_jaxpr/dot_general | solution.py:47
  239.8 5.4 %fusion.30 = f32[16,128,256]{1,2,0:T(8,128)} fusion(f32[16,128,256]{1,2,0:T(8,128)} %get-tuple-element.122, s32[]{:T(128)} %get-tuple-element.121, bf16[128,9216]{1,0:T(8,128)(2,1)S(1)} %get-tuple-element.132, s32[]{:T(128)} %get-tuple-element.131, s32[256]{0:T(256)S(1)} %add_multiply_fusion.2, s32[9216]{0:T(1024)S(1)} %iota_multiply_fusion.2), kind=kOutput, calls=%fused_computation.5.clone.1 | convolution fusion | flops 637009920 | bytes 2529280 | tf_op jit(solution)/shard_map/while/body/eval_jaxpr/dot_general | solution.py:47
  246.6 5.4 %fusion.30 = f32[16,128,256]{1,2,0:T(8,128)} fusion(f32[16,128,256]{1,2,0:T(8,128)} %get-tuple-element.122, s32[]{:T(128)} %get-tuple-element.121, bf16[128,9216]{1,0:T(8,128)(2,1)S(1)} %get-tuple-element.132, s32[]{:T(128)} %get-tuple-element.131, s32[256]{0:T(256)S(1)} %add_multiply_fusion.2, s32[9216]{0:T(1024)S(1)} %iota_multiply_fusion.2), kind=kOutput, calls=%fused_computation.5.clone.1 | convolution fusion | flops 637009920 | bytes 2529280 | tf_op jit(solution)/shard_map/while/body/eval_jaxpr/dot_general | solution.py:47
  253.4 5.4 %fusion.30 = f32[16,128,256]{1,2,0:T(8,128)} fusion(f32[16,128,256]{1,2,0:T(8,128)} %get-tuple-element.122, s32[]{:T(128)} %get-tuple-element.121, bf16[128,9216]{1,0:T(8,128)(2,1)S(1)} %get-tuple-element.132, s32[]{:T(128)} %get-tuple-element.131, s32[256]{0:T(256)S(1)} %add_multiply_fusion.2, s32[9216]{0:T(1024)S(1)} %iota_multiply_fusion.2), kind=kOutput, calls=%fused_computation.5.clone.1 | convolution fusion | flops 637009920 | bytes 2529280 | tf_op jit(solution)/shard_map/while/body/eval_jaxpr/dot_general | solution.py:47
  260.1 5.4 %fusion.30 = f32[16,128,256]{1,2,0:T(8,128)} fusion(f32[16,128,256]{1,2,0:T(8,128)} %get-tuple-element.122, s32[]{:T(128)} %get-tuple-element.121, bf16[128,9216]{1,0:T(8,128)(2,1)S(1)} %get-tuple-element.132, s32[]{:T(128)} %get-tuple-element.131, s32[256]{0:T(256)S(1)} %add_multiply_fusion.2, s32[9216]{0:T(1024)S(1)} %iota_multiply_fusion.2), kind=kOutput, calls=%fused_computation.5.clone.1 | convolution fusion | flops 637009920 | bytes 2529280 | tf_op jit(solution)/shard_map/while/body/eval_jaxpr/dot_general | solution.py:47
  266.9 5.4 %fusion.30 = f32[16,128,256]{1,2,0:T(8,128)} fusion(f32[16,128,256]{1,2,0:T(8,128)} %get-tuple-element.122, s32[]{:T(128)} %get-tuple-element.121, bf16[128,9216]{1,0:T(8,128)(2,1)S(1)} %get-tuple-element.132, s32[]{:T(128)} %get-tuple-element.131, s32[256]{0:T(256)S(1)} %add_multiply_fusion.2, s32[9216]{0:T(1024)S(1)} %iota_multiply_fusion.2), kind=kOutput, calls=%fused_computation.5.clone.1 | convolution fusion | flops 637009920 | bytes 2529280 | tf_op jit(solution)/shard_map/while/body/eval_jaxpr/dot_general | solution.py:47
  272.3 1.9 copy.26
  274.3 1.9 gather_fusion.1
  276.2 2.4 broadcast_select_fusion
  279.9 143.2 %all-reduce.3.cloned.1.call-done = f32[64,4096]{1,0:T(8,128)} async-done(((f32[64,4096]{1,0:T(8,128)}), f32[64,4096]{1,0:T(8,128)}) %all-reduce.3.cloned.1.call-update) | async-done | bytes 1048592
  423.1 1.5 dynamic-slice_multiply_fusion
  (67 shorter events, 8.8 us)
Async XLA Ops:
  6.5 2.5 copy-start
  25.7 47.9 %all-to-all-start = ((bf16[32,2,4096]{2,1,0:T(2,128)(2,1)}), bf16[32,2,4096]{2,1,0:T(2,128)(2,1)S(1)}, u32[]{:S(2)}, u32[]{:S(2)}) async-start(bf16[32,2,4096]{2,1,0:T(2,128)(2,1)} %reshape.154), calls=%async_computation | async-start | bytes 1048576 | tf_op jit(solution)/shard_map/all_to_all | solution.py:92
  54.4 28.8 %copy-start.1 = (s32[33]{0:T(128)S(1)}, s32[33]{0:T(128)}, u32[]{:S(2)}) copy-start(s32[33]{0:T(128)} %param.14) | copy-start | bytes 400
  73.6 10.6 %copy-start.2 = (s32[32]{0:T(128)S(1)}, s32[32]{0:T(128)}, u32[]{:S(2)}) copy-start(s32[32]{0:T(128)} %param.15) | copy-start | bytes 388
  73.6 52.4 %all-to-all-start.1 = ((bf16[32,2,14336]{2,1,0:T(2,128)(2,1)}), bf16[32,2,14336]{2,1,0:T(2,128)(2,1)S(1)}, u32[]{:S(2)}, u32[]{:S(2)}) async-start(bf16[32,2,14336]{2,1,0:T(2,128)(2,1)} %reshape.152), calls=%async_computation.1 | async-start | bytes 3670016 | tf_op jit(solution)/shard_map/all_to_all | solution.py:93
  83.0 340.1 %all-reduce.3.cloned.1.call-start = ((), (), s32[]{:S(2)}) async-start(), calls=%async_computation.2 | async-start | bytes 2097152
  274.3 4.3 %copy-start.3 = (u32[256]{0:T(256)S(1)}, u32[256]{0:T(256)}, u32[]{:S(2)}) copy-start(u32[256]{0:T(256)} %constant.121) | copy-start | bytes 3076
Sparse Core Ops, SparseCore 0:
  278.7 144.3 all-reduce.2
where the time goes:
time: 437 us; the launch traced here: 431 us
  waiting for transfers between devices  174 us (40%)
  local copies, waits for them, and re-layouts  109 us (25%)
  matrix products  94 us (22%)
  starting transfers between devices  21.4 us (5%)
  between operations  14.2 us (3%)
  loops' own time  11.3 us (3%)
  other arithmetic  7.23 us (2%)
    unnamed x2, waiting for transfers between devices  143 us
    dot_general x16, matrix products, one_panel(): lax.dot_general(vector, signs, (((1,), (1,)), ((), ())), preferred_elemen...  86.5 us
    unnamed x14, local copies, waits for them, and re-layouts  45.6 us
    all_to_all x1, waiting for transfers between devices, body(): lax.all_to_all(grad_b, 'cuts', split_axis=2, concat_axis=0, tiled=True)  30.7 us
    all_to_all x1, local copies, waits for them, and re-layouts, body(): lax.all_to_all(grad_b, 'cuts', split_axis=2, concat_axis=0, tiled=True)  19.1 us
    reshape x1, local copies, waits for them, and re-layouts, body(): grad_b = grad_b.astype(jnp.bfloat16).reshape(EXMAX, ADAPTER_RANK, -1)  14.1 us
    all_to_all x1, starting transfers between devices, body(): lax.all_to_all(grad_a, 'cuts', split_axis=2, concat_axis=0, tiled=True)  11.9 us
    another operation x1, loops' own time, sketch_rows(): pieces = lax.map(one_panel, jnp.arange(SKETCH // PANEL, dtype=jnp.int32))  11.3 us
  transfers between devices with their start and end apart: 3, of which 2 were waited for; matrix products, arithmetic and copies ran while one was open for 11% of the time, Pallas kernels for 0%

commit v1 on v0

v1 whole, which is shorter than its diff:
```python
import functools

import jax
import jax.numpy as jnp
import numpy as np
from jax import lax
from jax.experimental import pallas as pl
from jax.experimental.pallas import tpu as pltpu
from jax.sharding import Mesh
from jax.sharding import PartitionSpec as P

MODEL_WIDTH = 4096
HIDDEN_UNITS = 14336
RANK = 16
SKETCH = 4096
BLOCKS = 32
TOK_DEV = 128
EXMAX = 4
EXAMPLES = 64
NY, NCORE, NX, NZ = 4, 2, 4, 8
CHIPS = NY * NX
COLS = (MODEL_WIDTH + HIDDEN_UNITS) // CHIPS
ROWS = EXMAX * RANK
LANES = 128
TILES = COLS // LANES
A_WIDTH = MODEL_WIDTH // BLOCKS
B_WIDTH = HIDDEN_UNITS // BLOCKS
PAIRS = RANK // 2
SLOTS = NCORE * CHIPS * EXMAX
KDEV = SKETCH // NCORE
KTILE = KDEV // NX
CUT_SLOTS = NX * EXMAX
PIECES = NCORE * KTILE // LANES


def as_i32(value):
    value &= 0xFFFFFFFF
    return np.int32(value - (1 << 32) if value >= 1 << 31 else value)


Q_STEP = 1640531527
K_STEP = 668265263
MULT = as_i32(739982445 << 11)
NT = (((1,), (1,)), ((), ()))
F32 = jnp.float32
BF16 = jnp.bfloat16
I32 = jnp.int32


def iota(shape, dim):
    return lax.broadcasted_iota(I32, shape, dim)


def gradient_kernel(tok_ref, first_ref, cut_ref, act_ref, gout_ref, down_ref, up_ref, out_ref):
    up = lax.dot_general(gout_ref[...], up_ref[...], NT, preferred_element_type=F32).astype(BF16)
    down = jnp.dot(act_ref[...], down_ref[...], preferred_element_type=F32).astype(BF16)
    slot = tok_ref[...] - first_ref[cut_ref[0]]
    expand = (lax.rem(iota((ROWS, RANK), 0), RANK) == iota((ROWS, RANK), 1)).astype(F32).astype(BF16)
    mine = (iota((ROWS, TOK_DEV), 0) // RANK) == slot

    def spread(factor):
        rows = lax.dot_general(expand, factor, NT, preferred_element_type=F32)
        return jnp.where(mine, rows, 0.0).astype(BF16)

    spread_up, spread_down = spread(up), spread(down)
    for chip in range(CHIPS):
        lo, hi = chip * COLS, (chip + 1) * COLS
        mid = min(max(MODEL_WIDTH, lo), hi)
        if mid > lo:
            part = jnp.dot(spread_up, act_ref[:, lo:mid], preferred_element_type=F32)
            out_ref[chip, :, : mid - lo] = part.astype(BF16)
        if hi > mid:
            part = jnp.dot(
                spread_down,
                gout_ref[:, mid - MODEL_WIDTH : hi - MODEL_WIDTH],
                preferred_element_type=F32,
            )
            out_ref[chip, :, mid - lo :] = part.astype(BF16)


def sketch_kernel(where_ref, seeds_ref, own_ref, partner_ref, out_ref, vec_ref, base_ref, acc_ref):
    step = pl.program_id(0)
    chip, core = where_ref[0], where_ref[1]

    @pl.when(step == 0)
    def _():
        to, at = iota((256, 256), 0), iota((256, 256), 1)
        source = lax.rem(to, 16) // EXMAX * ROWS + lax.rem(to, EXMAX) * RANK + to // 16
        order = (at == source).astype(F32).astype(BF16)
        for half, ref in enumerate((own_ref, partner_ref)):
            for y in range(NY):
                rows = ref[NX * y : NX * (y + 1)].reshape(NX * ROWS, COLS)
                rows = jnp.dot(order, rows, preferred_element_type=F32).astype(BF16)
                lo = half * CHIPS * EXMAX + y * CUT_SLOTS
                for r in range(RANK):
                    vec_ref[r // 2, lo : lo + CUT_SLOTS, (r % 2) * COLS : (r % 2 + 1) * COLS] = rows[
                        r * CUT_SLOTS : (r + 1) * CUT_SLOTS
                    ]
        lane = iota((8, LANES), 1)
        for tile in range(TILES):
            column = chip * COLS + tile * LANES
            is_a = column < MODEL_WIDTH
            f = jnp.maximum(column - MODEL_WIDTH, 0)
            width = jnp.where(is_a, A_WIDTH, B_WIDTH)
            block = jnp.where(is_a, column // A_WIDTH, f // B_WIDTH)
            into = jnp.where(is_a, 0, f - f // B_WIDTH * B_WIDTH)
            after = jnp.minimum(block + 1, BLOCKS - 1)
            place = lane + into
            over = place >= width
            seed = jnp.where(over, seeds_ref[after], seeds_ref[block])
            place = jnp.where(over, place - width, place)
            start = jnp.where(is_a, 0, RANK * A_WIDTH)
            base = (place + start) * as_i32(Q_STEP) + seed
            for r in range(RANK):
                lo = (r % 2) * COLS + tile * LANES
                base_ref[r // 2, :, lo : lo + LANES] = base + (width * r) * as_i32(Q_STEP)

    feature = (iota((16, LANES), 0) + (core * KDEV + step * KTILE)) * as_i32(K_STEP)
    acc_ref[...] = jnp.zeros_like(acc_ref)

    def pair(p, carry):
        base = []
        for tile in range(2 * TILES):
            eight = base_ref[p, :, tile * LANES : (tile + 1) * LANES]
            base.append(jnp.concatenate([eight, eight], axis=0))
        rows = []
        for k in range(0, KTILE, 16):
            here = feature + as_i32(k * K_STEP)
            signs = []
            for tile in range(2 * TILES):
                h = base[tile] + here
                h = (h ^ lax.shift_right_logical(h, np.int32(15))) * MULT
                signs.append(jnp.where(h < 0, BF16(1), BF16(-1)))
            rows.append(jnp.concatenate(signs, axis=1))
        acc_ref[...] += lax.dot_general(
            jnp.concatenate(rows, axis=0), vec_ref[p], NT, preferred_element_type=F32
        )
        return carry

    lax.fori_loop(0, PAIRS, pair, 0)
    total = acc_ref[...].T.astype(BF16)
    for half in range(NCORE):
        to_core = core if half == 0 else 1 - core
        for y in range(NY):
            lo = half * CHIPS * EXMAX + y * CUT_SLOTS
            out_ref[y, to_core, 0] = total[lo : lo + CUT_SLOTS]


def route_kernel(first_ref, z_ref, in_ref, out_ref):
    sums = []
    for c in range(NCORE):
        total = jnp.zeros((CUT_SLOTS, KTILE), F32)
        for y in range(NY):
            for x in range(NX):
                total = total + in_ref[(y * NCORE + c) * NX + x].astype(F32)
        sums.append(total.astype(BF16))
    stacked = jnp.concatenate(
        [
            sums[c][:, u * LANES : (u + 1) * LANES]
            for c in range(NCORE)
            for u in range(KTILE // LANES)
        ],
        axis=0,
    )
    z = z_ref[0]
    width = PIECES * CUT_SLOTS
    row, col = iota((EXAMPLES * PIECES, width), 0), iota((EXAMPLES * PIECES, width), 1)
    slot = lax.rem(col, CUT_SLOTS)
    example = jnp.full(row.shape, -1, I32)
    for x in range(NX):
        cut = x * NZ + z
        number = first_ref[cut] + lax.rem(slot, EXMAX)
        number = jnp.where(number < first_ref[cut + 1], number, -1)
        example = jnp.where(slot // EXMAX == x, number, example)
    hit = (row // PIECES == example) & (lax.rem(row, PIECES) == col // CUT_SLOTS)
    routed = jnp.dot(hit.astype(F32).astype(BF16), stacked, preferred_element_type=F32)
    out_ref[...] = routed.astype(BF16).reshape(out_ref.shape)


def finish_kernel(in_ref, out_ref):
    scale = float(RANK * (MODEL_WIDTH + HIDDEN_UNITS) * TOK_DEV) ** (-0.5)
    per = KTILE // LANES
    for x in range(NX):
        total = jnp.zeros(in_ref.shape[1:], F32)
        for z in range(NZ):
            total = total + in_ref[x * NZ + z].astype(F32)
        total = total * scale
        for p in range(2):
            for c in range(NCORE):
                for u in range(per):
                    row = p * PIECES + c * per + u
                    lo = c * KDEV + x * KTILE + u * LANES
                    out_ref[p : p + 1, lo : lo + LANES] = total[row : row + 1]


VMEM = pl.BlockSpec(memory_space=pltpu.VMEM)
SMEM = pl.BlockSpec(memory_space=pltpu.SMEM)


def params(mib):
    return pltpu.CompilerParams(vmem_limit_bytes=mib << 20)


def body(acts, gouts, adapter_down, adapter_up, token_example, cut_first, seeds):
    y, core, x, z = (lax.axis_index(name) for name in ("y", "core", "x", "z"))
    cut = (x * NZ + z).astype(I32).reshape(1)
    grads = pl.pallas_call(
        gradient_kernel,
        out_shape=jax.ShapeDtypeStruct((CHIPS, ROWS, COLS), BF16),
        in_specs=[VMEM, SMEM, SMEM, VMEM, VMEM, VMEM, VMEM],
        out_specs=VMEM,
        compiler_params=params(40),
        name="gradients",
    )(token_example.reshape(1, TOK_DEV), cut_first, cut, acts, gouts, adapter_down, adapter_up)
    own = lax.all_to_all(grads, ("y", "x"), 0, 0, tiled=True)
    partner = lax.ppermute(own, "core", [(0, 1), (1, 0)])
    where = jnp.stack([(y * NX + x).astype(I32), core.astype(I32)])
    whole = lambda i: (0, 0, 0)
    parts = pl.pallas_call(
        sketch_kernel,
        grid=(NX,),
        out_shape=jax.ShapeDtypeStruct((NY, NCORE, NX, CUT_SLOTS, KTILE), BF16),
        in_specs=[
            SMEM,
            SMEM,
            pl.BlockSpec((CHIPS, ROWS, COLS), whole),
            pl.BlockSpec((CHIPS, ROWS, COLS), whole),
        ],
        out_specs=pl.BlockSpec((NY, NCORE, 1, CUT_SLOTS, KTILE), lambda i: (0, 0, i, 0, 0)),
        scratch_shapes=[
            pltpu.VMEM((PAIRS, SLOTS, 2 * COLS), BF16),
            pltpu.VMEM((PAIRS, 8, 2 * COLS), I32),
            pltpu.VMEM((KTILE, SLOTS), F32),
        ],
        compiler_params=params(48),
        name="sketch",
    )(where, seeds, own, partner)
    parts = parts.reshape(NY * NCORE * NX, CUT_SLOTS, KTILE)
    parts = lax.all_to_all(parts, ("y", "core", "x"), 0, 0, tiled=True)
    routed = pl.pallas_call(
        route_kernel,
        out_shape=jax.ShapeDtypeStruct((NX * NZ, 2 * PIECES, LANES), BF16),
        in_specs=[SMEM, SMEM, VMEM],
        out_specs=VMEM,
        compiler_params=params(32),
        name="route",
    )(cut_first, z.astype(I32).reshape(1), parts)
    routed = lax.all_to_all(routed, ("x", "z"), 0, 0, tiled=True)
    return pl.pallas_call(
        finish_kernel,
        out_shape=jax.ShapeDtypeStruct((2, SKETCH), F32),
        in_specs=[VMEM],
        out_specs=VMEM,
        compiler_params=params(32),
        name="finish",
    )(routed)


def solution(mesh):
    fine = Mesh(mesh.devices.reshape(NY, NCORE, NX, NZ), ("y", "core", "x", "z"))
    every = ("y", "core", "x", "z")
    in_specs = (P(every, None), P(every, None), P(), P(), P(every), P(("y", "core")), P())
    return jax.shard_map(body, mesh=fine, in_specs=in_specs, out_specs=P(every, None), check_vma=False)
```

time: 437 us -> 128 us (0.29); the launches traced: 431 us -> 127 us
  waiting for transfers between devices: 174 us -> 4.22 us
  local copies, waits for them, and re-layouts: 109 us -> 6.97 us
  matrix products: 94 us -> 0 us
  blocking collectives: 0 us -> 70.9 us
  Pallas kernels: 0 us -> 43.4 us
  starting transfers between devices: 21.4 us -> 1.8 us
  between operations: 14.2 us -> 0.06 us
  loops' own time: 11.3 us -> 0 us
  other arithmetic: 7.23 us -> 0.07 us
    unnamed x2 -> x0, waiting for transfers between devices: 143 us -> none
    dot_general x20 -> x0, matrix products: 94 us -> none  [the longest x16 86.5 us: one_panel(): lax.dot_general(vector, signs, (((1,), (1,)), ((), ())), preferred_elemen...]
    all_to_all x0 -> x3, blocking collectives: none -> 70.9 us  [the longest x1 37.7 us: body(): own = lax.all_to_all(grads, ('y', 'x'), 0, 0, tiled=True)]
    pallas_call x0 -> x4, Pallas kernels: none -> 43.4 us  [the longest x1 37.8 us: body(): pl.pallas_call(sketch_kernel, grid=(NX,), out_shape=jax.ShapeDtypeStruct(...]
    unnamed x14 -> x15, local copies, waits for them, and re-layouts: 45.6 us -> 6.97 us
    all_to_all x2 -> x0, waiting for transfers between devices: 30.7 us -> none  [the longest x1 30.7 us: body(): lax.all_to_all(grad_b, 'cuts', split_axis=2, concat_axis=0, tiled=True)]
    all_to_all x2 -> x0, local copies, waits for them, and re-layouts: 24.4 us -> none  [the longest x1 19.1 us: body(): lax.all_to_all(grad_b, 'cuts', split_axis=2, concat_axis=0, tiled=True)]
    reshape x4 -> x0, local copies, waits for them, and re-layouts: 24 us -> none  [the longest x1 14.1 us: body(): grad_b = grad_b.astype(jnp.bfloat16).reshape(EXMAX, ADAPTER_RANK, -1)]
  transfers between devices with their start and end apart: 3 -> 1, of which waited for: 2 -> 1; matrix products, arithmetic and copies ran while one was open for 11% -> 0% of each run, Pallas kernels for 0% -> 0%
where the time goes in v1:
time: 128 us; the launch traced here: 127 us
  blocking collectives  70.9 us (55%)
  Pallas kernels  43.4 us (34%)
  local copies, waits for them, and re-layouts  6.97 us (5%)
  waiting for transfers between devices  4.22 us (3%)
  starting transfers between devices  1.8 us (1%)
    pallas_call x1, Pallas kernels, body(): pl.pallas_call(sketch_kernel, grid=(NX,), out_shape=jax.ShapeDtypeStruct(...  37.8 us
    all_to_all x1, blocking collectives, body(): own = lax.all_to_all(grads, ('y', 'x'), 0, 0, tiled=True)  37.7 us
    all_to_all x1, blocking collectives, body(): routed = lax.all_to_all(routed, ('x', 'z'), 0, 0, tiled=True)  18.4 us
    all_to_all x1, blocking collectives, body(): parts = lax.all_to_all(parts, ('y', 'core', 'x'), 0, 0, tiled=True)  14.7 us
    unnamed x15, local copies, waits for them, and re-layouts  6.97 us
    ppermute x1, waiting for transfers between devices, body(): partner = lax.ppermute(own, 'core', [(0, 1), (1, 0)])  4.22 us
    pallas_call x1, Pallas kernels, body(): pl.pallas_call(gradient_kernel, out_shape=jax.ShapeDtypeStruct((CHIPS, RO...  4.12 us
  transfers between devices with their start and end apart: 1, of which 1 were waited for; matrix products, arithmetic and copies ran while one was open for 0% of the time, Pallas kernels for 0%

profile of v1, /device:TPU:1, one launch (start us, length us, event | category | flops | bytes accessed | tf_op | source)
XLA Modules:
  0.0 127.4 jit_solution(6488841846825007344)
XLA Ops:
  0.0 1.4 %copy.8.down_ref = bf16[4096,16]{1,0:T(8,128)(2,1)S(1)} copy(bf16[4096,16]{0,1:T(8,128)(2,1)} %param.9) | data formatting | bytes 262144 | tf_op args[2]
  1.4 0.0 copy-start
  1.4 2.0 %copy-done = bf16[128,14336]{1,0:T(8,128)(2,1)S(1)} copy-done((bf16[128,14336]{1,0:T(8,128)(2,1)S(1)}, bf16[128,14336]{1,0:T(8,128)(2,1)}, u32[]{:S(2)}) %copy-start) | copy-done | bytes 3670040
  3.4 0.0 copy-start.1
  3.4 1.2 copy-done.1
  4.7 0.0 copy-start.2
  4.7 1.0 copy-done.2
  5.7 0.0 copy-start.3
  5.7 0.7 copy-done.3
  6.3 0.0 copy-start.5
  6.3 0.7 copy-done.5
  7.0 4.1 %gradients.1 = bf16[16,64,1152]{2,1,0:T(8,128)(2,1)S(1)} custom-call(s32[1,128]{1,0:T(1,128)S(1)} %bitcast.7, s32[33]{0:T(128)S(1)} %copy-done.3, s32[1]{0:T(128)} %bitcast.4.cut_ref, bf16[128,4096]{1,0:T(8,128)(2,1)S(1)} %copy-done.1, bf16[128,14336]{1,0:T(8,128)(2,1)S(1)} %copy-done, bf16[4096,16]{1,0:T(8,128)(2,1)S(1)} %copy.8.down_ref, ...), custom_call_target="tpu_custom_call" | custom-call | tf_op jit(solution)/shard_map/gradients/pallas_call | solution.py:207
  11.1 0.0 copy-start.6
  11.1 37.7 %all_to_all.15.own_ref = bf16[16,64,1152]{2,1,0:T(8,128)(2,1)S(1)} all-to-all(bf16[16,64,1152]{2,1,0:T(8,128)(2,1)S(1)} %gradients.1), channel_id=1, replica_groups=mesh['y'=4,'core'=2,'x'=4,'z'=8] {'y','x'}, dimensions={0} | all-to-all | bytes 4718592 | tf_op jit(solution)/shard_map/all_to_all | solution.py:215
  48.9 1.8 %collective-permute-start = (bf16[16,64,1152]{2,1,0:T(8,128)(2,1)S(1)}, bf16[16,64,1152]{2,1,0:T(8,128)(2,1)}, u32[]{:S(2)}, u32[]{:S(2)}) collective-permute-start(bf16[16,64,1152]{2,1,0:T(8,128)(2,1)S(1)} %all_to_all.15.own_ref), channel_id=1, source_target_pairs={{0,32},{32,0},{1,33},{33,1},{2,34},{34,2},{3,35},{35,3},{4,36},{36... | collective-permute-start | bytes 7077896 | tf_op jit(solution)/shard_map/ppermute | solution.py:216
  50.7 0.1 pad_add_fusion.where_ref
  50.7 0.0 copy-start.4
  50.7 4.2 %collective-permute-done.partner_ref = bf16[16,64,1152]{2,1,0:T(8,128)(2,1)} collective-permute-done((bf16[16,64,1152]{2,1,0:T(8,128)(2,1)S(1)}, bf16[16,64,1152]{2,1,0:T(8,128)(2,1)}, u32[]{:S(2)}, u32[]{:S(2)}) %collective-permute-start) | collective-permute-done | bytes 2359328 | tf_op jit(solution)/shard_map/ppermute | solution.py:216
  55.0 0.0 copy-done.6
  55.0 37.8 %sketch.1 = bf16[4,2,4,16,512]{4,3,2,1,0:T(8,128)(2,1)S(1)} custom-call(s32[2]{0:T(128)S(1)} %pad_add_fusion.where_ref, s32[32]{0:T(128)S(1)} %copy-done.6, bf16[16,64,1152]{2,1,0:T(8,128)(2,1)S(1)} %all_to_all.15.own_ref, bf16[16,64,1152]{2,1,0:T(8,128)(2,1)} %collective-permute-done.partner_ref), custom_call_target="tpu_custom_call" | custom-call | tf_op jit(solution)/shard_map/sketch/pallas_call | solution.py:219
  92.8 14.7 %all_to_all.16.in_ref = bf16[32,16,512]{2,1,0:T(8,128)(2,1)S(1)} all-to-all(bf16[32,16,512]{2,1,0:T(8,128)(2,1)S(1)} %bitcast.6), channel_id=1, replica_groups=mesh['y'=4,'core'=2,'x'=4,'z'=8] {'y','core','x'}, dimensions={0} | all-to-all | bytes 1048576 | tf_op jit(solution)/shard_map/all_to_all | solution.py:239
  107.5 0.0 copy-done.4
  107.5 0.8 route.1
  108.3 18.4 %all_to_all.17.in_ref = bf16[32,16,128]{2,1,0:T(8,128)(2,1)S(1)} all-to-all(bf16[32,16,128]{2,1,0:T(8,128)(2,1)S(1)} %route.1), channel_id=1, replica_groups=mesh['y'=4,'core'=2,'x'=4,'z'=8] {'x','z'}, dimensions={0} | all-to-all | bytes 262144 | tf_op jit(solution)/shard_map/all_to_all | solution.py:248
  126.7 0.6 finish.1
Async XLA Ops:
  1.4 2.0 %copy-start = (bf16[128,14336]{1,0:T(8,128)(2,1)S(1)}, bf16[128,14336]{1,0:T(8,128)(2,1)}, u32[]{:S(2)}) copy-start(bf16[128,14336]{1,0:T(8,128)(2,1)} %gout_ref.1) | copy-start | bytes 11010052
  3.4 1.2 copy-start.1
  4.7 1.0 copy-start.2
  5.7 0.7 copy-start.3
  6.3 0.7 copy-start.5
  11.1 43.8 %copy-start.6 = (s32[32]{0:T(128)S(1)}, s32[32]{0:T(128)}, u32[]{:S(2)}) copy-start(s32[32]{0:T(128)} %seeds_ref.1) | copy-start | bytes 388
  48.9 6.1 %collective-permute-start = (bf16[16,64,1152]{2,1,0:T(8,128)(2,1)S(1)}, bf16[16,64,1152]{2,1,0:T(8,128)(2,1)}, u32[]{:S(2)}, u32[]{:S(2)}) collective-permute-start(bf16[16,64,1152]{2,1,0:T(8,128)(2,1)S(1)} %all_to_all.15.own_ref), channel_id=1, source_target_pairs={{0,32},{32,0},{1,33},{33,1},{2,34},{34,2},{3,35},{35,3},{4,36},{36... | collective-permute-start | bytes 7077896 | tf_op jit(solution)/shard_map/ppermute | solution.py:216
  50.7 56.8 %copy-start.4 = (s32[33]{0:T(128)S(1)}, s32[33]{0:T(128)}, u32[]{:S(2)}) copy-start(s32[33]{0:T(128)} %first_ref.3) | copy-start | bytes 400

commit v2 on v1

v2 whole, which is shorter than its diff:
```python
import jax
import jax.numpy as jnp
import numpy as np
from jax import lax
from jax.experimental import pallas as pl
from jax.experimental.pallas import tpu as pltpu
from jax.sharding import Mesh
from jax.sharding import PartitionSpec as P

MODEL_WIDTH = 4096
HIDDEN_UNITS = 14336
RANK = 16
SKETCH = 4096
BLOCKS = 32
TOK_DEV = 128
EXMAX = 4
EXAMPLES = 64
NY, NCORE, NX, NZ = 4, 2, 4, 8
CHIPS = NY * NX
COLS = (MODEL_WIDTH + HIDDEN_UNITS) // CHIPS
ROWS = EXMAX * RANK
LANES = 128
TILES = COLS // LANES
A_WIDTH = MODEL_WIDTH // BLOCKS
B_WIDTH = HIDDEN_UNITS // BLOCKS
PAIRS = RANK // 2
SLOTS = NCORE * CHIPS * EXMAX
KDEV = SKETCH // NCORE
KTILE = KDEV // NX
CUT_SLOTS = NX * EXMAX
PIECES = NCORE * KTILE // LANES
GROUPS = (3, 6, 9, 13, 16)
EARLY = PAIRS // 2


def as_i32(value):
    value &= 0xFFFFFFFF
    return np.int32(value - (1 << 32) if value >= 1 << 31 else value)


Q_STEP = 1640531527
K_STEP = 668265263
MULT = as_i32(739982445 << 11)
NT = (((1,), (1,)), ((), ()))
F32 = jnp.float32
BF16 = jnp.bfloat16
I32 = jnp.int32


def iota(shape, dim):
    return lax.broadcasted_iota(I32, shape, dim)


def gradient_kernel(
    tok_hbm, first_hbm, act_hbm, gout_hbm, down_hbm, up_hbm, out_ref,
    tok_ref, first_ref, act_ref, gout_ref, down_ref, up_ref, sems,
):
    copies = [
        pltpu.make_async_copy(src, dst, sems.at[i])
        for i, (src, dst) in enumerate(
            (
                (down_hbm, down_ref),
                (act_hbm, act_ref),
                (tok_hbm, tok_ref),
                (first_hbm, first_ref),
                (up_hbm, up_ref),
            )
        )
    ]
    for lo, hi in zip(GROUPS[:-1], GROUPS[1:]):
        columns = slice(max(lo * COLS - MODEL_WIDTH, 0), hi * COLS - MODEL_WIDTH)
        copies.append(
            pltpu.make_async_copy(
                gout_hbm.at[:, columns], gout_ref.at[:, columns], sems.at[len(copies)]
            )
        )
    for copy in copies:
        copy.start()
    expand = (lax.rem(iota((ROWS, RANK), 0), RANK) == iota((ROWS, RANK), 1)).astype(F32).astype(BF16)
    for copy in copies[:4]:
        copy.wait()
    cut = lax.axis_index("x") * NZ + lax.axis_index("z")
    slot = tok_ref[...] - first_ref[cut]
    mine = (iota((ROWS, TOK_DEV), 0) // RANK) == slot

    def spread(factor):
        rows = lax.dot_general(expand, factor.astype(BF16), NT, preferred_element_type=F32)
        return jnp.where(mine, rows, 0.0).astype(BF16)

    spread_down = spread(
        lax.dot_general(act_ref[...], down_ref[...], NT, preferred_element_type=F32)
    )
    copies[4].wait()
    up = jnp.zeros((TOK_DEV, RANK), F32)
    for group, (first, last) in enumerate(zip(GROUPS[:-1], GROUPS[1:])):
        copies[5 + group].wait()
        for chip in range(first, last):
            lo, hi = max(chip * COLS - MODEL_WIDTH, 0), (chip + 1) * COLS - MODEL_WIDTH
            up = up + lax.dot_general(
                gout_ref[:, lo:hi], up_ref[:, lo:hi], NT, preferred_element_type=F32
            )
            part = jnp.dot(spread_down, gout_ref[:, lo:hi], preferred_element_type=F32)
            out_ref[chip, :, COLS - (hi - lo) :] = part.astype(BF16)
    spread_up = spread(up)
    for chip in range(GROUPS[0] + 1):
        lo, hi = chip * COLS, min((chip + 1) * COLS, MODEL_WIDTH)
        part = jnp.dot(spread_up, act_ref[:, lo:hi], preferred_element_type=F32)
        out_ref[chip, :, : hi - lo] = part.astype(BF16)


def signs_of(base_ref, p, feature):
    base = []
    for tile in range(2 * TILES):
        eight = base_ref[p, :, tile * LANES : (tile + 1) * LANES]
        base.append(jnp.concatenate([eight, eight], axis=0))
    for k in range(0, KTILE, 16):
        here = feature + as_i32(k * K_STEP)
        signs = []
        for tile in range(2 * TILES):
            h = base[tile] + here
            h = (h ^ lax.shift_right_logical(h, np.int32(15))) * MULT
            signs.append(jnp.where(h < 0, BF16(1), BF16(-1)))
        yield k, jnp.concatenate(signs, axis=1)


def first_feature(core, step):
    return (iota((16, LANES), 0) + (core * KDEV + step * KTILE)) * as_i32(K_STEP)


def sign_kernel(where_ref, seeds_ref, base_ref, sign_hbm, made_ref, sems):
    chip, core = where_ref[0], where_ref[1]
    lane = iota((8, LANES), 1)
    for tile in range(TILES):
        column = chip * COLS + tile * LANES
        is_a = column < MODEL_WIDTH
        f = jnp.maximum(column - MODEL_WIDTH, 0)
        width = jnp.where(is_a, A_WIDTH, B_WIDTH)
        block = jnp.where(is_a, column // A_WIDTH, f // B_WIDTH)
        into = jnp.where(is_a, 0, f - f // B_WIDTH * B_WIDTH)
        after = jnp.minimum(block + 1, BLOCKS - 1)
        place = lane + into
        over = place >= width
        seed = jnp.where(over, seeds_ref[after], seeds_ref[block])
        place = jnp.where(over, place - width, place)
        start = jnp.where(is_a, 0, RANK * A_WIDTH)
        base = (place + start) * as_i32(Q_STEP) + seed
        for r in range(RANK):
            lo = (r % 2) * COLS + tile * LANES
            base_ref[r // 2, :, lo : lo + LANES] = base + (width * r) * as_i32(Q_STEP)

    def send(i):
        slot = lax.rem(i, 2)
        return pltpu.make_async_copy(made_ref.at[slot], sign_hbm.at[i], sems.at[slot])

    def fill(i, carry):
        @pl.when(i >= 2)
        def _():
            send(i - 2).wait()

        slot = lax.rem(i, 2)
        tile, p = i // EARLY, lax.rem(i, EARLY)
        for k, signs in signs_of(base_ref, p, first_feature(core, tile)):
            made_ref[slot, k : k + 16] = signs
        send(i).start()
        return carry

    lax.fori_loop(0, NX * EARLY, fill, 0)
    send(NX * EARLY - 2).wait()
    send(NX * EARLY - 1).wait()


def sketch_kernel(
    where_ref, base_ref, sign_hbm, own_ref, partner_ref, out_ref, vec_ref, acc_ref, sign_ref, sems
):
    core = where_ref[1]

    def fetch(i):
        slot = lax.rem(i, 3)
        return pltpu.make_async_copy(sign_hbm.at[i], sign_ref.at[slot], sems.at[slot])

    fetch(0).start()
    fetch(1).start()
    to, at = iota((256, 256), 0), iota((256, 256), 1)
    source = lax.rem(to, 16) // EXMAX * ROWS + lax.rem(to, EXMAX) * RANK + to // 16
    order = (at == source).astype(F32).astype(BF16)
    for half, ref in enumerate((own_ref, partner_ref)):
        for y in range(NY):
            rows = ref[NX * y : NX * (y + 1)].reshape(NX * ROWS, COLS)
            rows = jnp.dot(order, rows, preferred_element_type=F32).astype(BF16)
            lo = half * CHIPS * EXMAX + y * CUT_SLOTS
            for r in range(RANK):
                vec_ref[r // 2, lo : lo + CUT_SLOTS, (r % 2) * COLS : (r % 2 + 1) * COLS] = rows[
                    r * CUT_SLOTS : (r + 1) * CUT_SLOTS
                ]

    def tile(step, carry):
        feature = first_feature(core, step)
        acc_ref[...] = jnp.zeros_like(acc_ref)

        def pair(i, carry):
            n = step * EARLY + i

            @pl.when(n + 2 < NX * EARLY)
            def _():
                fetch(n + 2).start()

            fetch(n).wait()
            early = lax.dot_general(
                sign_ref[lax.rem(n, 3)], vec_ref[i], NT, preferred_element_type=F32
            )
            late = jnp.concatenate([rows for _, rows in signs_of(base_ref, EARLY + i, feature)], axis=0)
            late = lax.dot_general(late, vec_ref[EARLY + i], NT, preferred_element_type=F32)
            acc_ref[...] += early + late
            return carry

        lax.fori_loop(0, EARLY, pair, 0)
        total = acc_ref[...].T.astype(BF16)
        for half in range(NCORE):
            to_core = core if half == 0 else 1 - core
            for y in range(NY):
                lo = half * CHIPS * EXMAX + y * CUT_SLOTS
                out_ref[y, to_core, step] = total[lo : lo + CUT_SLOTS]
        return carry

    lax.fori_loop(0, NX, tile, 0)


def route_kernel(first_ref, z_ref, in_ref, out_ref):
    sums = []
    for c in range(NCORE):
        total = jnp.zeros((CUT_SLOTS, KTILE), F32)
        for y in range(NY):
            for x in range(NX):
                total = total + in_ref[(y * NCORE + c) * NX + x].astype(F32)
        sums.append(total.astype(BF16))
    stacked = jnp.concatenate(
        [
            sums[c][:, u * LANES : (u + 1) * LANES]
            for c in range(NCORE)
            for u in range(KTILE // LANES)
        ],
        axis=0,
    )
    z = z_ref[0]
    width = PIECES * CUT_SLOTS
    row, col = iota((EXAMPLES * PIECES, width), 0), iota((EXAMPLES * PIECES, width), 1)
    slot = lax.rem(col, CUT_SLOTS)
    example = jnp.full(row.shape, -1, I32)
    for x in range(NX):
        cut = x * NZ + z
        number = first_ref[cut] + lax.rem(slot, EXMAX)
        number = jnp.where(number < first_ref[cut + 1], number, -1)
        example = jnp.where(slot // EXMAX == x, number, example)
    hit = (row // PIECES == example) & (lax.rem(row, PIECES) == col // CUT_SLOTS)
    routed = jnp.dot(hit.astype(F32).astype(BF16), stacked, preferred_element_type=F32)
    out_ref[...] = routed.astype(BF16).reshape(out_ref.shape)


def finish_kernel(in_ref, out_ref):
    scale = float(RANK * (MODEL_WIDTH + HIDDEN_UNITS) * TOK_DEV) ** (-0.5)
    per = KTILE // LANES
    for x in range(NX):
        total = jnp.zeros(in_ref.shape[1:], F32)
        for z in range(NZ):
            total = total + in_ref[x * NZ + z].astype(F32)
        total = total * scale
        for p in range(2):
            for c in range(NCORE):
                for u in range(per):
                    row = p * PIECES + c * per + u
                    lo = c * KDEV + x * KTILE + u * LANES
                    out_ref[p : p + 1, lo : lo + LANES] = total[row : row + 1]


VMEM = pl.BlockSpec(memory_space=pltpu.VMEM)
SMEM = pl.BlockSpec(memory_space=pltpu.SMEM)
HBM = pl.BlockSpec(memory_space=pltpu.HBM)


def in_hbm(array):
    return pltpu.with_memory_space_constraint(array, pltpu.HBM)


def params(mib):
    return pltpu.CompilerParams(vmem_limit_bytes=mib << 20)


def body(acts, gouts, adapter_down, adapter_up, token_example, cut_first, seeds):
    y, core, x, z = (lax.axis_index(name) for name in ("y", "core", "x", "z"))
    grads = pl.pallas_call(
        gradient_kernel,
        out_shape=pltpu.HBM((CHIPS, ROWS, COLS), BF16),
        in_specs=[HBM] * 6,
        out_specs=VMEM,
        scratch_shapes=[
            pltpu.VMEM((1, TOK_DEV), I32),
            pltpu.SMEM((cut_first.shape[0],), I32),
            pltpu.VMEM(acts.shape, BF16),
            pltpu.VMEM(gouts.shape, BF16),
            pltpu.VMEM((RANK, MODEL_WIDTH), BF16),
            pltpu.VMEM(adapter_up.shape, BF16),
            pltpu.SemaphoreType.DMA((5 + len(GROUPS) - 1,)),
        ],
        compiler_params=params(16),
        name="gradients",
    )(*(in_hbm(a) for a in (token_example.reshape(1, TOK_DEV), cut_first, acts, gouts, adapter_down.T, adapter_up)))
    where = jnp.stack([(y * NX + x).astype(I32), core.astype(I32)])
    where, seeds, grads = lax.optimization_barrier((where, seeds, grads))
    own = lax.all_to_all(grads, ("y", "x"), 0, 0, tiled=True)
    base, early = pl.pallas_call(
        sign_kernel,
        out_shape=(
            pltpu.VMEM((PAIRS, 8, 2 * COLS), I32),
            pltpu.HBM((NX * EARLY, KTILE, 2 * COLS), BF16),
        ),
        in_specs=[SMEM, SMEM],
        out_specs=(VMEM, HBM),
        scratch_shapes=[
            pltpu.VMEM((2, KTILE, 2 * COLS), BF16),
            pltpu.SemaphoreType.DMA((2,)),
        ],
        cost_estimate=pl.CostEstimate(flops=20_000_000_000, bytes_accessed=0, transcendentals=0),
        compiler_params=params(16),
        name="signs",
    )(where, seeds)
    own, base = lax.optimization_barrier((own, base))
    partner = lax.ppermute(own, "core", [(0, 1), (1, 0)])
    parts = pl.pallas_call(
        sketch_kernel,
        out_shape=jax.ShapeDtypeStruct((NY, NCORE, NX, CUT_SLOTS, KTILE), BF16),
        in_specs=[SMEM, VMEM, HBM, VMEM, VMEM],
        out_specs=VMEM,
        scratch_shapes=[
            pltpu.VMEM((PAIRS, SLOTS, 2 * COLS), BF16),
            pltpu.VMEM((KTILE, SLOTS), F32),
            pltpu.VMEM((3, KTILE, 2 * COLS), BF16),
            pltpu.SemaphoreType.DMA((3,)),
        ],
        compiler_params=params(32),
        name="sketch",
    )(where, base, in_hbm(early), own, partner)
    parts = parts.reshape(NY * NCORE * NX, CUT_SLOTS, KTILE)
    parts = lax.all_to_all(parts, ("y", "core", "x"), 0, 0, tiled=True)
    routed = pl.pallas_call(
        route_kernel,
        out_shape=jax.ShapeDtypeStruct((NX * NZ, 2 * PIECES, LANES), BF16),
        in_specs=[SMEM, SMEM, VMEM],
        out_specs=VMEM,
        compiler_params=params(32),
        name="route",
    )(cut_first, z.astype(I32).reshape(1), parts)
    routed = lax.all_to_all(routed, ("x", "z"), 0, 0, tiled=True)
    return pl.pallas_call(
        finish_kernel,
        out_shape=jax.ShapeDtypeStruct((2, SKETCH), F32),
        in_specs=[VMEM],
        out_specs=VMEM,
        compiler_params=params(32),
        name="finish",
    )(routed)


def solution(mesh):
    fine = Mesh(mesh.devices.reshape(NY, NCORE, NX, NZ), ("y", "core", "x", "z"))
    every = ("y", "core", "x", "z")
    in_specs = (P(every, None), P(every, None), P(), P(), P(every), P(("y", "core")), P())
    return jax.shard_map(body, mesh=fine, in_specs=in_specs, out_specs=P(every, None), check_vma=False)
```

time: 128 us -> 122 us (0.953)
  blocking collectives: 70.9 us -> 18.4 us
  waiting for transfers between devices: 4.22 us -> 29.5 us
  Pallas kernels: 43.4 us -> 59.8 us
  starting transfers between devices: 1.8 us -> 13.7 us
  local copies, waits for them, and re-layouts: 6.97 us -> 0.01 us
    all_to_all x2 -> x0, blocking collectives: 52.5 us -> none  [the longest x1 37.7 us: body(): own = lax.all_to_all(grads, ('y', 'x'), 0, 0, tiled=True)]
    all_to_all x0 -> x2, waiting for transfers between devices: none -> 25.4 us  [the longest x1 14 us: body(): own = lax.all_to_all(grads, ('y', 'x'), 0, 0, tiled=True)]
    pallas_call x2 -> x3, Pallas kernels: 42 us -> 58.3 us  [the longest x1 31.5 us: body(): pl.pallas_call(sketch_kernel, out_shape=jax.ShapeDtypeStruct((NY, NCORE,...]
    all_to_all x0 -> x2, starting transfers between devices: none -> 11.8 us  [the longest x1 7.59 us: body(): own = lax.all_to_all(grads, ('y', 'x'), 0, 0, tiled=True)]
    unnamed x15 -> x4, local copies, waits for them, and re-layouts: 6.97 us -> 0.01 us
  transfers between devices with their start and end apart: 1 -> 3, of which waited for: 1 -> 3; matrix products, arithmetic and copies ran while one was open for 0% -> 0% of each run, Pallas kernels for 0% -> 17%
where the time goes in v2:
time: 122 us
  Pallas kernels  59.8 us (49%)
  waiting for transfers between devices  29.5 us (24%)
  blocking collectives  18.4 us (15%)
  starting transfers between devices  13.7 us (11%)
    pallas_call x1, Pallas kernels, body(): pl.pallas_call(sketch_kernel, out_shape=jax.ShapeDtypeStruct((NY, NCORE,...  31.5 us
    pallas_call x1, Pallas kernels, body(): pl.pallas_call(sign_kernel, out_shape=(pltpu.VMEM((PAIRS, 8, 2 * COLS), I...  20.6 us
    all_to_all x1, blocking collectives, body(): routed = lax.all_to_all(routed, ('x', 'z'), 0, 0, tiled=True)  18.4 us
    all_to_all x1, waiting for transfers between devices, body(): own = lax.all_to_all(grads, ('y', 'x'), 0, 0, tiled=True)  14 us
    all_to_all x1, waiting for transfers between devices, body(): parts = lax.all_to_all(parts, ('y', 'core', 'x'), 0, 0, tiled=True)  11.4 us
    all_to_all x1, starting transfers between devices, body(): own = lax.all_to_all(grads, ('y', 'x'), 0, 0, tiled=True)  7.59 us
    pallas_call x1, Pallas kernels, body(): pl.pallas_call(gradient_kernel, out_shape=pltpu.HBM((CHIPS, ROWS, COLS),...  6.26 us
    all_to_all x1, starting transfers between devices, body(): parts = lax.all_to_all(parts, ('y', 'core', 'x'), 0, 0, tiled=True)  4.24 us
  transfers between devices with their start and end apart: 3, of which 3 were waited for; matrix products, arithmetic and copies ran while one was open for 0% of the time, Pallas kernels for 17%

profile of v2, /device:TPU:1, one launch (start us, length us, event | category | flops | bytes accessed | tf_op | source)
XLA Modules:
  0.0 121.6 jit_solution(789105832106804733)
XLA Ops:
  0.0 0.1 pad_add_fusion.where_ref
  0.1 6.3 %gradients.1 = bf16[16,64,1152]{2,1,0:T(8,128)(2,1)} custom-call(s32[1,128]{1,0:T(1,128)} %bitcast.7, s32[33]{0:T(128)} %first_ref.1, bf16[128,4096]{1,0:T(8,128)(2,1)} %act_hbm.1, bf16[128,14336]{1,0:T(8,128)(2,1)} %gout_hbm.1, bf16[16,4096]{1,0:T(8,128)(2,1)} %bitcast.6, bf16[16,14336]{1,0:T(8,128)(2,1)} %up_hbm.1), custom_call_target="tpu_custom_call" | custom-call | tf_op jit(solution)/shard_map/gradients/pallas_call | solution.py:290
  6.3 0.0 copy-start.1
  6.4 7.6 %all-to-all-start = ((bf16[16,64,1152]{2,1,0:T(8,128)(2,1)}), bf16[16,64,1152]{2,1,0:T(8,128)(2,1)S(1)}, u32[]{:S(2)}, u32[]{:S(2)}) async-start(bf16[16,64,1152]{2,1,0:T(8,128)(2,1)} %gradients.1), calls=%async_computation | async-start | bytes 4718592 | tf_op jit(solution)/shard_map/all_to_all | solution.py:309
  14.0 0.0 copy-done.1
  14.0 20.6 %signs.1 = (s32[8,8,2304]{2,1,0:T(8,128)S(1)}, bf16[16,512,2304]{2,1,0:T(8,128)(2,1)}) custom-call(s32[2]{0:T(128)S(1)} %pad_add_fusion.where_ref, s32[32]{0:T(128)S(1)} %copy-done.1), custom_call_target="tpu_custom_call" | custom-call | flops 20000000000 | tf_op jit(solution)/shard_map/signs/pallas_call | solution.py:310
  34.6 14.0 %all-to-all-done.own_ref = bf16[16,64,1152]{2,1,0:T(8,128)(2,1)S(1)} async-done(((bf16[16,64,1152]{2,1,0:T(8,128)(2,1)}), bf16[16,64,1152]{2,1,0:T(8,128)(2,1)S(1)}, u32[]{:S(2)}, u32[]{:S(2)}) %all-to-all-start) | async-done | bytes 2359328 | tf_op jit(solution)/shard_map/all_to_all | solution.py:309
  48.6 1.8 %collective-permute-start = (bf16[16,64,1152]{2,1,0:T(8,128)(2,1)S(1)}, bf16[16,64,1152]{2,1,0:T(8,128)(2,1)S(1)}, u32[]{:S(2)}, u32[]{:S(2)}) collective-permute-start(bf16[16,64,1152]{2,1,0:T(8,128)(2,1)S(1)} %all-to-all-done.own_ref), channel_id=1, source_target_pairs={{0,32},{32,0},{1,33},{33,1},{2,34},{34,2},{3,35},{35,3},{4,36},{36... | collective-permute-start | bytes 7077896 | tf_op jit(solution)/shard_map/ppermute | solution.py:327
  50.4 4.2 %collective-permute-done.partner_ref = bf16[16,64,1152]{2,1,0:T(8,128)(2,1)S(1)} collective-permute-done((bf16[16,64,1152]{2,1,0:T(8,128)(2,1)S(1)}, bf16[16,64,1152]{2,1,0:T(8,128)(2,1)S(1)}, u32[]{:S(2)}, u32[]{:S(2)}) %collective-permute-start) | collective-permute-done | bytes 2359328 | tf_op jit(solution)/shard_map/ppermute | solution.py:327
  54.6 0.0 copy-start
  54.6 31.5 %sketch.1 = bf16[4,2,4,16,512]{4,3,2,1,0:T(8,128)(2,1)} custom-call(s32[2]{0:T(128)S(1)} %pad_add_fusion.where_ref, s32[8,8,2304]{2,1,0:T(8,128)S(1)} %get-tuple-element.16.base_ref, bf16[16,512,2304]{2,1,0:T(8,128)(2,1)} %get-tuple-element.17.sign_hbm, bf16[16,64,1152]{2,1,0:T(8,128)(2,1)S(1)} %all-to-all-done.own_ref, ...), custom_call_target="tpu_custom_call" | custom-call | tf_op jit(solution)/shard_map/sketch/pallas_call | solution.py:328
  86.0 4.2 %all-to-all-start.1 = ((bf16[32,16,512]{2,1,0:T(8,128)(2,1)}), bf16[32,16,512]{2,1,0:T(8,128)(2,1)S(1)}, u32[]{:S(2)}, u32[]{:S(2)}) async-start(bf16[32,16,512]{2,1,0:T(8,128)(2,1)} %bitcast.5), calls=%async_computation.1 | async-start | bytes 1048576 | tf_op jit(solution)/shard_map/all_to_all | solution.py:343
  90.3 11.4 %all-to-all-done.1.in_ref = bf16[32,16,512]{2,1,0:T(8,128)(2,1)S(1)} async-done(((bf16[32,16,512]{2,1,0:T(8,128)(2,1)}), bf16[32,16,512]{2,1,0:T(8,128)(2,1)S(1)}, u32[]{:S(2)}, u32[]{:S(2)}) %all-to-all-start.1) | async-done | bytes 524320 | tf_op jit(solution)/shard_map/all_to_all | solution.py:343
  101.7 0.0 copy-done
  101.7 0.8 route.1
  102.5 18.4 %all_to_all.15.in_ref = bf16[32,16,128]{2,1,0:T(8,128)(2,1)S(1)} all-to-all(bf16[32,16,128]{2,1,0:T(8,128)(2,1)S(1)} %route.1), channel_id=1, replica_groups=mesh['y'=4,'core'=2,'x'=4,'z'=8] {'x','z'}, dimensions={0} | all-to-all | bytes 262144 | tf_op jit(solution)/shard_map/all_to_all | solution.py:352
  120.9 0.6 finish.1
Async XLA Ops:
  6.3 7.6 %copy-start.1 = (s32[32]{0:T(128)S(1)}, s32[32]{0:T(128)}, u32[]{:S(2)}) copy-start(s32[32]{0:T(128)} %seeds_ref) | copy-start | bytes 388
  6.4 42.2 %all-to-all-start = ((bf16[16,64,1152]{2,1,0:T(8,128)(2,1)}), bf16[16,64,1152]{2,1,0:T(8,128)(2,1)S(1)}, u32[]{:S(2)}, u32[]{:S(2)}) async-start(bf16[16,64,1152]{2,1,0:T(8,128)(2,1)} %gradients.1), calls=%async_computation | async-start | bytes 4718592 | tf_op jit(solution)/shard_map/all_to_all | solution.py:309
  48.6 6.0 %collective-permute-start = (bf16[16,64,1152]{2,1,0:T(8,128)(2,1)S(1)}, bf16[16,64,1152]{2,1,0:T(8,128)(2,1)S(1)}, u32[]{:S(2)}, u32[]{:S(2)}) collective-permute-start(bf16[16,64,1152]{2,1,0:T(8,128)(2,1)S(1)} %all-to-all-done.own_ref), channel_id=1, source_target_pairs={{0,32},{32,0},{1,33},{33,1},{2,34},{34,2},{3,35},{35,3},{4,36},{36... | collective-permute-start | bytes 7077896 | tf_op jit(solution)/shard_map/ppermute | solution.py:327
  54.6 47.1 %copy-start = (s32[33]{0:T(128)S(1)}, s32[33]{0:T(128)}, u32[]{:S(2)}) copy-start(s32[33]{0:T(128)} %first_ref.1) | copy-start | bytes 400
  86.0 15.6 %all-to-all-start.1 = ((bf16[32,16,512]{2,1,0:T(8,128)(2,1)}), bf16[32,16,512]{2,1,0:T(8,128)(2,1)S(1)}, u32[]{:S(2)}, u32[]{:S(2)}) async-start(bf16[32,16,512]{2,1,0:T(8,128)(2,1)} %bitcast.5), calls=%async_computation.1 | async-start | bytes 1048576 | tf_op jit(solution)/shard_map/all_to_all | solution.py:343

commit v3 on v2

--- a/solution.py
+++ b/solution.py
@@ -52,8 +52,8 @@
 
 
 def gradient_kernel(
-    tok_hbm, first_hbm, act_hbm, gout_hbm, down_hbm, up_hbm, out_ref,
-    tok_ref, first_ref, act_ref, gout_ref, down_ref, up_ref, sems,
+    tok_hbm, first_hbm, act_hbm, gout_hbm, down_hbm, up_hbm, out_hbm,
+    tok_ref, first_ref, act_ref, gout_ref, down_ref, up_ref, made_ref, sems, sent,
 ):
     copies = [
         pltpu.make_async_copy(src, dst, sems.at[i])
@@ -91,6 +91,9 @@
         lax.dot_general(act_ref[...], down_ref[...], NT, preferred_element_type=F32)
     )
     copies[4].wait()
+    def send(chip):
+        return pltpu.make_async_copy(made_ref.at[chip], out_hbm.at[chip], sent.at[chip])
+
     up = jnp.zeros((TOK_DEV, RANK), F32)
     for group, (first, last) in enumerate(zip(GROUPS[:-1], GROUPS[1:])):
         copies[5 + group].wait()
@@ -100,53 +103,62 @@
                 gout_ref[:, lo:hi], up_ref[:, lo:hi], NT, preferred_element_type=F32
             )
             part = jnp.dot(spread_down, gout_ref[:, lo:hi], preferred_element_type=F32)
-            out_ref[chip, :, COLS - (hi - lo) :] = part.astype(BF16)
+            made_ref[chip, :, COLS - (hi - lo) :] = part.astype(BF16)
+            if chip > GROUPS[0]:
+                send(chip).start()
     spread_up = spread(up)
     for chip in range(GROUPS[0] + 1):
         lo, hi = chip * COLS, min((chip + 1) * COLS, MODEL_WIDTH)
         part = jnp.dot(spread_up, act_ref[:, lo:hi], preferred_element_type=F32)
-        out_ref[chip, :, : hi - lo] = part.astype(BF16)
-
-
-def signs_of(base_ref, p, feature):
-    base = []
-    for tile in range(2 * TILES):
-        eight = base_ref[p, :, tile * LANES : (tile + 1) * LANES]
-        base.append(jnp.concatenate([eight, eight], axis=0))
-    for k in range(0, KTILE, 16):
-        here = feature + as_i32(k * K_STEP)
-        signs = []
-        for tile in range(2 * TILES):
-            h = base[tile] + here
-            h = (h ^ lax.shift_right_logical(h, np.int32(15))) * MULT
-            signs.append(jnp.where(h < 0, BF16(1), BF16(-1)))
-        yield k, jnp.concatenate(signs, axis=1)
+        made_ref[chip, :, : hi - lo] = part.astype(BF16)
+        send(chip).start()
+    for chip in range(CHIPS):
+        send(chip).wait()
+
+
+def width_of(chip, tile):
+    return jnp.where(chip * COLS + tile * LANES < MODEL_WIDTH, A_WIDTH, B_WIDTH)
+
+
+def signs_of(base_ref, chip, p, feature):
+    for half in range(2):
+        for tile in range(TILES):
+            shift = width_of(chip, tile) * (2 * p + half) * as_i32(Q_STEP)
+            there = [
+                feature + (as_i32(k * K_STEP) + shift) for k in range(0, KTILE, LANES)
+            ]
+            for row in range(tile * LANES, (tile + 1) * LANES, 16):
+                base = base_ref[row : row + 16]
+                signs = []
+                for here in there:
+                    h = base + here
+                    h = (h ^ lax.shift_right_logical(h, np.int32(15))) * MULT
+                    signs.append(jnp.where(h < 0, BF16(1), BF16(-1)))
+                yield half * COLS + row, jnp.concatenate(signs, axis=1)
 
 
 def first_feature(core, step):
-    return (iota((16, LANES), 0) + (core * KDEV + step * KTILE)) * as_i32(K_STEP)
+    return (iota((16, LANES), 1) + (core * KDEV + step * KTILE)) * as_i32(K_STEP)
 
 
 def sign_kernel(where_ref, seeds_ref, base_ref, sign_hbm, made_ref, sems):
     chip, core = where_ref[0], where_ref[1]
-    lane = iota((8, LANES), 1)
+    row = iota((LANES, LANES), 0)
     for tile in range(TILES):
         column = chip * COLS + tile * LANES
         is_a = column < MODEL_WIDTH
         f = jnp.maximum(column - MODEL_WIDTH, 0)
-        width = jnp.where(is_a, A_WIDTH, B_WIDTH)
+        width = width_of(chip, tile)
         block = jnp.where(is_a, column // A_WIDTH, f // B_WIDTH)
         into = jnp.where(is_a, 0, f - f // B_WIDTH * B_WIDTH)
         after = jnp.minimum(block + 1, BLOCKS - 1)
-        place = lane + into
+        place = row + into
         over = place >= width
         seed = jnp.where(over, seeds_ref[after], seeds_ref[block])
         place = jnp.where(over, place - width, place)
         start = jnp.where(is_a, 0, RANK * A_WIDTH)
         base = (place + start) * as_i32(Q_STEP) + seed
-        for r in range(RANK):
-            lo = (r % 2) * COLS + tile * LANES
-            base_ref[r // 2, :, lo : lo + LANES] = base + (width * r) * as_i32(Q_STEP)
+        base_ref[tile * LANES : (tile + 1) * LANES] = base
 
     def send(i):
         slot = lax.rem(i, 2)
@@ -159,8 +171,8 @@
 
         slot = lax.rem(i, 2)
         tile, p = i // EARLY, lax.rem(i, EARLY)
-        for k, signs in signs_of(base_ref, p, first_feature(core, tile)):
-            made_ref[slot, k : k + 16] = signs
+        for row, signs in signs_of(base_ref, chip, p, first_feature(core, tile)):
+            made_ref[slot, row : row + 16] = signs
         send(i).start()
         return carry
 
@@ -172,7 +184,7 @@
 def sketch_kernel(
     where_ref, base_ref, sign_hbm, own_ref, partner_ref, out_ref, vec_ref, acc_ref, sign_ref, sems
 ):
-    core = where_ref[1]
+    chip, core = where_ref[0], where_ref[1]
 
     def fetch(i):
         slot = lax.rem(i, 3)
@@ -205,16 +217,15 @@
                 fetch(n + 2).start()
 
             fetch(n).wait()
-            early = lax.dot_general(
-                sign_ref[lax.rem(n, 3)], vec_ref[i], NT, preferred_element_type=F32
-            )
-            late = jnp.concatenate([rows for _, rows in signs_of(base_ref, EARLY + i, feature)], axis=0)
-            late = lax.dot_general(late, vec_ref[EARLY + i], NT, preferred_element_type=F32)
+            early = jnp.dot(vec_ref[i], sign_ref[lax.rem(n, 3)], preferred_element_type=F32)
+            late = [signs for _, signs in signs_of(base_ref, chip, EARLY + i, feature)]
+            late = jnp.concatenate(late, axis=0)
+            late = jnp.dot(vec_ref[EARLY + i], late, preferred_element_type=F32)
             acc_ref[...] += early + late
             return carry
 
         lax.fori_loop(0, EARLY, pair, 0)
-        total = acc_ref[...].T.astype(BF16)
+        total = acc_ref[...].astype(BF16)
         for half in range(NCORE):
             to_core = core if half == 0 else 1 - core
             for y in range(NY):
@@ -291,7 +302,7 @@
         gradient_kernel,
         out_shape=pltpu.HBM((CHIPS, ROWS, COLS), BF16),
         in_specs=[HBM] * 6,
-        out_specs=VMEM,
+        out_specs=HBM,
         scratch_shapes=[
             pltpu.VMEM((1, TOK_DEV), I32),
             pltpu.SMEM((cut_first.shape[0],), I32),
@@ -299,7 +310,9 @@
             pltpu.VMEM(gouts.shape, BF16),
             pltpu.VMEM((RANK, MODEL_WIDTH), BF16),
             pltpu.VMEM(adapter_up.shape, BF16),
+            pltpu.VMEM((CHIPS, ROWS, COLS), BF16),
             pltpu.SemaphoreType.DMA((5 + len(GROUPS) - 1,)),
+            pltpu.SemaphoreType.DMA((CHIPS,)),
         ],
         compiler_params=params(16),
         name="gradients",
@@ -310,13 +323,13 @@
     base, early = pl.pallas_call(
         sign_kernel,
         out_shape=(
-            pltpu.VMEM((PAIRS, 8, 2 * COLS), I32),
-            pltpu.HBM((NX * EARLY, KTILE, 2 * COLS), BF16),
+            pltpu.VMEM((COLS, LANES), I32),
+            pltpu.HBM((NX * EARLY, 2 * COLS, KTILE), BF16),
         ),
         in_specs=[SMEM, SMEM],
         out_specs=(VMEM, HBM),
         scratch_shapes=[
-            pltpu.VMEM((2, KTILE, 2 * COLS), BF16),
+            pltpu.VMEM((2, 2 * COLS, KTILE), BF16),
             pltpu.SemaphoreType.DMA((2,)),
         ],
         cost_estimate=pl.CostEstimate(flops=20_000_000_000, bytes_accessed=0, transcendentals=0),
@@ -332,8 +345,8 @@
         out_specs=VMEM,
         scratch_shapes=[
             pltpu.VMEM((PAIRS, SLOTS, 2 * COLS), BF16),
-            pltpu.VMEM((KTILE, SLOTS), F32),
-            pltpu.VMEM((3, KTILE, 2 * COLS), BF16),
+            pltpu.VMEM((SLOTS, KTILE), F32),
+            pltpu.VMEM((3, 2 * COLS, KTILE), BF16),
             pltpu.SemaphoreType.DMA((3,)),
         ],
         compiler_params=params(32),

time: 122 us -> 118 us (0.967)
  Pallas kernels: 59.8 us -> 56.4 us
    pallas_call x1, Pallas kernels: 31.5 us -> 28.5 us  [body(): pl.pallas_call(sketch_kernel, out_shape=jax.ShapeDtypeStruct((NY, NCORE,...]
  transfers between devices with their start and end apart: 3 -> 3, of which waited for: 3 -> 3; matrix products, arithmetic and copies ran while one was open for 0% -> 0% of each run, Pallas kernels for 17% -> 18%
where the time goes in v3:
time: 118 us
  Pallas kernels  56.4 us (48%)
  waiting for transfers between devices  29.5 us (25%)
  blocking collectives  18.4 us (16%)
  starting transfers between devices  13.6 us (12%)
    pallas_call x1, Pallas kernels, body(): pl.pallas_call(sketch_kernel, out_shape=jax.ShapeDtypeStruct((NY, NCORE,...  28.5 us
    pallas_call x1, Pallas kernels, body(): pl.pallas_call(sign_kernel, out_shape=(pltpu.VMEM((COLS, LANES), I32), pl...  20.7 us
    all_to_all x1, blocking collectives, body(): routed = lax.all_to_all(routed, ('x', 'z'), 0, 0, tiled=True)  18.4 us
    all_to_all x1, waiting for transfers between devices, body(): own = lax.all_to_all(grads, ('y', 'x'), 0, 0, tiled=True)  14 us
    all_to_all x1, waiting for transfers between devices, body(): parts = lax.all_to_all(parts, ('y', 'core', 'x'), 0, 0, tiled=True)  11.4 us
    all_to_all x1, starting transfers between devices, body(): own = lax.all_to_all(grads, ('y', 'x'), 0, 0, tiled=True)  7.6 us
    pallas_call x1, Pallas kernels, body(): pl.pallas_call(gradient_kernel, out_shape=pltpu.HBM((CHIPS, ROWS, COLS),...  5.75 us
    all_to_all x1, starting transfers between devices, body(): parts = lax.all_to_all(parts, ('y', 'core', 'x'), 0, 0, tiled=True)  4.22 us
  transfers between devices with their start and end apart: 3, of which 3 were waited for; matrix products, arithmetic and copies ran while one was open for 0% of the time, Pallas kernels for 18%

profile of v3, /device:TPU:1, one launch (start us, length us, event | category | flops | bytes accessed | tf_op | source)
XLA Modules:
  0.0 118.1 jit_solution(16578088885396193561)
XLA Ops:
  0.0 0.1 pad_add_fusion.where_ref
  0.1 5.8 %gradients.1 = bf16[16,64,1152]{2,1,0:T(8,128)(2,1)} custom-call(s32[1,128]{1,0:T(1,128)} %bitcast.7, s32[33]{0:T(128)} %first_ref.1, bf16[128,4096]{1,0:T(8,128)(2,1)} %act_hbm.1, bf16[128,14336]{1,0:T(8,128)(2,1)} %gout_hbm.1, bf16[16,4096]{1,0:T(8,128)(2,1)} %bitcast.6, bf16[16,14336]{1,0:T(8,128)(2,1)} %up_hbm.1), custom_call_target="tpu_custom_call" | custom-call | tf_op jit(solution)/shard_map/gradients/pallas_call | solution.py:301
  5.8 0.0 copy-start.1
  5.8 7.6 %all-to-all-start = ((bf16[16,64,1152]{2,1,0:T(8,128)(2,1)}), bf16[16,64,1152]{2,1,0:T(8,128)(2,1)S(1)}, u32[]{:S(2)}, u32[]{:S(2)}) async-start(bf16[16,64,1152]{2,1,0:T(8,128)(2,1)} %gradients.1), calls=%async_computation | async-start | bytes 4718592 | tf_op jit(solution)/shard_map/all_to_all | solution.py:322
  13.5 0.0 copy-done.1
  13.5 20.7 %signs.1 = (s32[1152,128]{1,0:T(8,128)S(1)}, bf16[16,2304,512]{2,1,0:T(8,128)(2,1)}) custom-call(s32[2]{0:T(128)S(1)} %pad_add_fusion.where_ref, s32[32]{0:T(128)S(1)} %copy-done.1), custom_call_target="tpu_custom_call" | custom-call | flops 20000000000 | tf_op jit(solution)/shard_map/signs/pallas_call | solution.py:323
  34.1 14.0 %all-to-all-done.own_ref = bf16[16,64,1152]{2,1,0:T(8,128)(2,1)S(1)} async-done(((bf16[16,64,1152]{2,1,0:T(8,128)(2,1)}), bf16[16,64,1152]{2,1,0:T(8,128)(2,1)S(1)}, u32[]{:S(2)}, u32[]{:S(2)}) %all-to-all-start) | async-done | bytes 2359328 | tf_op jit(solution)/shard_map/all_to_all | solution.py:322
  48.1 1.8 %collective-permute-start = (bf16[16,64,1152]{2,1,0:T(8,128)(2,1)S(1)}, bf16[16,64,1152]{2,1,0:T(8,128)(2,1)S(1)}, u32[]{:S(2)}, u32[]{:S(2)}) collective-permute-start(bf16[16,64,1152]{2,1,0:T(8,128)(2,1)S(1)} %all-to-all-done.own_ref), channel_id=1, source_target_pairs={{0,32},{32,0},{1,33},{33,1},{2,34},{34,2},{3,35},{35,3},{4,36},{36... | collective-permute-start | bytes 7077896 | tf_op jit(solution)/shard_map/ppermute | solution.py:340
  49.9 4.2 %collective-permute-done.partner_ref = bf16[16,64,1152]{2,1,0:T(8,128)(2,1)S(1)} collective-permute-done((bf16[16,64,1152]{2,1,0:T(8,128)(2,1)S(1)}, bf16[16,64,1152]{2,1,0:T(8,128)(2,1)S(1)}, u32[]{:S(2)}, u32[]{:S(2)}) %collective-permute-start) | collective-permute-done | bytes 2359328 | tf_op jit(solution)/shard_map/ppermute | solution.py:340
  54.1 0.0 copy-start
  54.1 28.5 %sketch.1 = bf16[4,2,4,16,512]{4,3,2,1,0:T(8,128)(2,1)} custom-call(s32[2]{0:T(128)S(1)} %pad_add_fusion.where_ref, s32[1152,128]{1,0:T(8,128)S(1)} %get-tuple-element.16.base_ref, bf16[16,2304,512]{2,1,0:T(8,128)(2,1)} %get-tuple-element.17.sign_hbm, bf16[16,64,1152]{2,1,0:T(8,128)(2,1)S(1)} %all-to-all-done.own_ref, ...), custom_call_target="tpu_custom_call" | custom-call | tf_op jit(solution)/shard_map/sketch/pallas_call | solution.py:341
  82.6 4.2 %all-to-all-start.1 = ((bf16[32,16,512]{2,1,0:T(8,128)(2,1)}), bf16[32,16,512]{2,1,0:T(8,128)(2,1)S(1)}, u32[]{:S(2)}, u32[]{:S(2)}) async-start(bf16[32,16,512]{2,1,0:T(8,128)(2,1)} %bitcast.5), calls=%async_computation.1 | async-start | bytes 1048576 | tf_op jit(solution)/shard_map/all_to_all | solution.py:356
  86.9 11.4 %all-to-all-done.1.in_ref = bf16[32,16,512]{2,1,0:T(8,128)(2,1)S(1)} async-done(((bf16[32,16,512]{2,1,0:T(8,128)(2,1)}), bf16[32,16,512]{2,1,0:T(8,128)(2,1)S(1)}, u32[]{:S(2)}, u32[]{:S(2)}) %all-to-all-start.1) | async-done | bytes 524320 | tf_op jit(solution)/shard_map/all_to_all | solution.py:356
  98.3 0.0 copy-done
  98.3 0.8 route.1
  99.1 18.4 %all_to_all.15.in_ref = bf16[32,16,128]{2,1,0:T(8,128)(2,1)S(1)} all-to-all(bf16[32,16,128]{2,1,0:T(8,128)(2,1)S(1)} %route.1), channel_id=1, replica_groups=mesh['y'=4,'core'=2,'x'=4,'z'=8] {'x','z'}, dimensions={0} | all-to-all | bytes 262144 | tf_op jit(solution)/shard_map/all_to_all | solution.py:365
  117.5 0.6 finish.1
Async XLA Ops:
  5.8 7.6 %copy-start.1 = (s32[32]{0:T(128)S(1)}, s32[32]{0:T(128)}, u32[]{:S(2)}) copy-start(s32[32]{0:T(128)} %seeds_ref) | copy-start | bytes 388
  5.8 42.2 %all-to-all-start = ((bf16[16,64,1152]{2,1,0:T(8,128)(2,1)}), bf16[16,64,1152]{2,1,0:T(8,128)(2,1)S(1)}, u32[]{:S(2)}, u32[]{:S(2)}) async-start(bf16[16,64,1152]{2,1,0:T(8,128)(2,1)} %gradients.1), calls=%async_computation | async-start | bytes 4718592 | tf_op jit(solution)/shard_map/all_to_all | solution.py:322
  48.1 6.0 %collective-permute-start = (bf16[16,64,1152]{2,1,0:T(8,128)(2,1)S(1)}, bf16[16,64,1152]{2,1,0:T(8,128)(2,1)S(1)}, u32[]{:S(2)}, u32[]{:S(2)}) collective-permute-start(bf16[16,64,1152]{2,1,0:T(8,128)(2,1)S(1)} %all-to-all-done.own_ref), channel_id=1, source_target_pairs={{0,32},{32,0},{1,33},{33,1},{2,34},{34,2},{3,35},{35,3},{4,36},{36... | collective-permute-start | bytes 7077896 | tf_op jit(solution)/shard_map/ppermute | solution.py:340
  54.1 44.2 %copy-start = (s32[33]{0:T(128)S(1)}, s32[33]{0:T(128)}, u32[]{:S(2)}) copy-start(s32[33]{0:T(128)} %first_ref.1) | copy-start | bytes 400
  82.6 15.6 %all-to-all-start.1 = ((bf16[32,16,512]{2,1,0:T(8,128)(2,1)}), bf16[32,16,512]{2,1,0:T(8,128)(2,1)S(1)}, u32[]{:S(2)}, u32[]{:S(2)}) async-start(bf16[32,16,512]{2,1,0:T(8,128)(2,1)} %bitcast.5), calls=%async_computation.1 | async-start | bytes 1048576 | tf_op jit(solution)/shard_map/all_to_all | solution.py:356

commit v4 on v3

--- a/solution.py
+++ b/solution.py
@@ -30,6 +30,7 @@
 CUT_SLOTS = NX * EXMAX
 PIECES = NCORE * KTILE // LANES
 GROUPS = (3, 6, 9, 13, 16)
+DEPTH = 256
 EARLY = PAIRS // 2
 
 
@@ -181,50 +182,64 @@
     send(NX * EARLY - 1).wait()
 
 
-def sketch_kernel(
-    where_ref, base_ref, sign_hbm, own_ref, partner_ref, out_ref, vec_ref, acc_ref, sign_ref, sems
-):
-    chip, core = where_ref[0], where_ref[1]
-
-    def fetch(i):
-        slot = lax.rem(i, 3)
-        return pltpu.make_async_copy(sign_hbm.at[i], sign_ref.at[slot], sems.at[slot])
-
-    fetch(0).start()
-    fetch(1).start()
+def arrange(ref, vec_ref):
     to, at = iota((256, 256), 0), iota((256, 256), 1)
     source = lax.rem(to, 16) // EXMAX * ROWS + lax.rem(to, EXMAX) * RANK + to // 16
     order = (at == source).astype(F32).astype(BF16)
-    for half, ref in enumerate((own_ref, partner_ref)):
-        for y in range(NY):
-            rows = ref[NX * y : NX * (y + 1)].reshape(NX * ROWS, COLS)
-            rows = jnp.dot(order, rows, preferred_element_type=F32).astype(BF16)
-            lo = half * CHIPS * EXMAX + y * CUT_SLOTS
-            for r in range(RANK):
-                vec_ref[r // 2, lo : lo + CUT_SLOTS, (r % 2) * COLS : (r % 2 + 1) * COLS] = rows[
-                    r * CUT_SLOTS : (r + 1) * CUT_SLOTS
-                ]
+    for y in range(NY):
+        rows = ref[NX * y : NX * (y + 1)].reshape(NX * ROWS, COLS)
+        rows = jnp.dot(order, rows, preferred_element_type=F32).astype(BF16)
+        lo = y * CUT_SLOTS
+        for r in range(RANK):
+            vec_ref[r // 2, lo : lo + CUT_SLOTS, (r % 2) * COLS : (r % 2 + 1) * COLS] = rows[
+                r * CUT_SLOTS : (r + 1) * CUT_SLOTS
+            ]
+
+
+def arrange_kernel(in_ref, out_ref):
+    arrange(in_ref, out_ref)
+
+
+def sketch_kernel(
+    where_ref, base_ref, sign_hbm, mine_ref, partner_ref, out_ref, vec_ref, acc_ref, sign_ref, sems
+):
+    chip, core = where_ref[0], where_ref[1]
+
+    def fetch(i):
+        slot = lax.rem(i, 2 * EARLY)
+        return pltpu.make_async_copy(sign_hbm.at[i], sign_ref.at[slot], sems.at[slot])
+
+    for i in range(EARLY):
+        fetch(i).start()
+    arrange(partner_ref, vec_ref)
+
+    def vectors(p, q):
+        return jnp.concatenate(
+            [mine_ref[p, :, q : q + DEPTH], vec_ref[p, :, q : q + DEPTH]], axis=0
+        )
 
     def tile(step, carry):
         feature = first_feature(core, step)
         acc_ref[...] = jnp.zeros_like(acc_ref)
 
+        @pl.when(step + 1 < NX)
+        def _():
+            for i in range(EARLY):
+                fetch((step + 1) * EARLY + i).start()
+
         def pair(i, carry):
             n = step * EARLY + i
-
-            @pl.when(n + 2 < NX * EARLY)
-            def _():
-                fetch(n + 2).start()
-
+            slot = lax.rem(n, 2 * EARLY)
             fetch(n).wait()
-            early = jnp.dot(vec_ref[i], sign_ref[lax.rem(n, 3)], preferred_element_type=F32)
-            late = [signs for _, signs in signs_of(base_ref, chip, EARLY + i, feature)]
-            late = jnp.concatenate(late, axis=0)
-            late = jnp.dot(vec_ref[EARLY + i], late, preferred_element_type=F32)
-            acc_ref[...] += early + late
+            made = signs_of(base_ref, chip, EARLY + i, feature)
+            for q in range(0, 2 * COLS, DEPTH):
+                late = jnp.concatenate([next(made)[1] for _ in range(DEPTH // 16)], axis=0)
+                acc_ref[...] += jnp.dot(
+                    vectors(i, q), sign_ref[slot, q : q + DEPTH], preferred_element_type=F32
+                ) + jnp.dot(vectors(EARLY + i, q), late, preferred_element_type=F32)
             return carry
 
-        lax.fori_loop(0, EARLY, pair, 0)
+        lax.fori_loop(0, EARLY, pair, 0, unroll=True)
         total = acc_ref[...].astype(BF16)
         for half in range(NCORE):
             to_core = core if half == 0 else 1 - core
@@ -338,20 +353,29 @@
     )(where, seeds)
     own, base = lax.optimization_barrier((own, base))
     partner = lax.ppermute(own, "core", [(0, 1), (1, 0)])
+    mine = pl.pallas_call(
+        arrange_kernel,
+        out_shape=jax.ShapeDtypeStruct((PAIRS, SLOTS // NCORE, 2 * COLS), BF16),
+        in_specs=[VMEM],
+        out_specs=VMEM,
+        cost_estimate=pl.CostEstimate(flops=1_500_000_000, bytes_accessed=0, transcendentals=0),
+        compiler_params=params(16),
+        name="arrange",
+    )(own)
     parts = pl.pallas_call(
         sketch_kernel,
         out_shape=jax.ShapeDtypeStruct((NY, NCORE, NX, CUT_SLOTS, KTILE), BF16),
         in_specs=[SMEM, VMEM, HBM, VMEM, VMEM],
         out_specs=VMEM,
         scratch_shapes=[
-            pltpu.VMEM((PAIRS, SLOTS, 2 * COLS), BF16),
+            pltpu.VMEM((PAIRS, SLOTS // NCORE, 2 * COLS), BF16),
             pltpu.VMEM((SLOTS, KTILE), F32),
-            pltpu.VMEM((3, 2 * COLS, KTILE), BF16),
-            pltpu.SemaphoreType.DMA((3,)),
+            pltpu.VMEM((2 * EARLY, 2 * COLS, KTILE), BF16),
+            pltpu.SemaphoreType.DMA((2 * EARLY,)),
         ],
         compiler_params=params(32),
         name="sketch",
-    )(where, base, in_hbm(early), own, partner)
+    )(where, base, in_hbm(early), mine, partner)
     parts = parts.reshape(NY * NCORE * NX, CUT_SLOTS, KTILE)
     parts = lax.all_to_all(parts, ("y", "core", "x"), 0, 0, tiled=True)
     routed = pl.pallas_call(

time: 118 us -> 112 us (0.949)
  Pallas kernels: 56.4 us -> 51.3 us
    pallas_call x1, Pallas kernels: 28.5 us -> 22.6 us  [body(): pl.pallas_call(sketch_kernel, out_shape=jax.ShapeDtypeStruct((NY, NCORE,...]
  transfers between devices with their start and end apart: 3 -> 3, of which waited for: 3 -> 3; matrix products, arithmetic and copies ran while one was open for 0% -> 0% of each run, Pallas kernels for 18% -> 19%
where the time goes in v4:
time: 112 us
  Pallas kernels  51.3 us (46%)
  waiting for transfers between devices  28.6 us (26%)
  blocking collectives  18.4 us (16%)
  starting transfers between devices  13.6 us (12%)
    pallas_call x1, Pallas kernels, body(): pl.pallas_call(sketch_kernel, out_shape=jax.ShapeDtypeStruct((NY, NCORE,...  22.6 us
    pallas_call x1, Pallas kernels, body(): pl.pallas_call(sign_kernel, out_shape=(pltpu.VMEM((COLS, LANES), I32), pl...  20.7 us
    all_to_all x1, blocking collectives, body(): routed = lax.all_to_all(routed, ('x', 'z'), 0, 0, tiled=True)  18.4 us
    all_to_all x1, waiting for transfers between devices, body(): own = lax.all_to_all(grads, ('y', 'x'), 0, 0, tiled=True)  14 us
    all_to_all x1, waiting for transfers between devices, body(): parts = lax.all_to_all(parts, ('y', 'core', 'x'), 0, 0, tiled=True)  11.4 us
    all_to_all x1, starting transfers between devices, body(): own = lax.all_to_all(grads, ('y', 'x'), 0, 0, tiled=True)  7.6 us
    pallas_call x1, Pallas kernels, body(): pl.pallas_call(gradient_kernel, out_shape=pltpu.HBM((CHIPS, ROWS, COLS),...  5.75 us
    all_to_all x1, starting transfers between devices, body(): parts = lax.all_to_all(parts, ('y', 'core', 'x'), 0, 0, tiled=True)  4.21 us
  transfers between devices with their start and end apart: 3, of which 3 were waited for; matrix products, arithmetic and copies ran while one was open for 0% of the time, Pallas kernels for 19%

profile of v4, /device:TPU:1, one launch (start us, length us, event | category | flops | bytes accessed | tf_op | source)
XLA Modules:
  0.0 112.2 jit_solution(10714235804996309547)
XLA Ops:
  0.0 0.1 pad_add_fusion.where_ref
  0.1 5.8 %gradients.1 = bf16[16,64,1152]{2,1,0:T(8,128)(2,1)} custom-call(s32[1,128]{1,0:T(1,128)} %bitcast.7, s32[33]{0:T(128)} %first_ref.1, bf16[128,4096]{1,0:T(8,128)(2,1)} %act_hbm.1, bf16[128,14336]{1,0:T(8,128)(2,1)} %gout_hbm.1, bf16[16,4096]{1,0:T(8,128)(2,1)} %bitcast.6, bf16[16,14336]{1,0:T(8,128)(2,1)} %up_hbm.1), custom_call_target="tpu_custom_call" | custom-call | tf_op jit(solution)/shard_map/gradients/pallas_call | solution.py:316
  5.8 0.0 copy-start.1
  5.8 7.6 %all-to-all-start = ((bf16[16,64,1152]{2,1,0:T(8,128)(2,1)}), bf16[16,64,1152]{2,1,0:T(8,128)(2,1)S(1)}, u32[]{:S(2)}, u32[]{:S(2)}) async-start(bf16[16,64,1152]{2,1,0:T(8,128)(2,1)} %gradients.1), calls=%async_computation | async-start | bytes 4718592 | tf_op jit(solution)/shard_map/all_to_all | solution.py:337
  13.5 0.0 copy-done.1
  13.5 20.7 %signs.1 = (s32[1152,128]{1,0:T(8,128)S(1)}, bf16[16,2304,512]{2,1,0:T(8,128)(2,1)}) custom-call(s32[2]{0:T(128)S(1)} %pad_add_fusion.where_ref, s32[32]{0:T(128)S(1)} %copy-done.1), custom_call_target="tpu_custom_call" | custom-call | flops 20000000000 | tf_op jit(solution)/shard_map/signs/pallas_call | solution.py:338
  34.1 14.0 %all-to-all-done.in_ref = bf16[16,64,1152]{2,1,0:T(8,128)(2,1)S(1)} async-done(((bf16[16,64,1152]{2,1,0:T(8,128)(2,1)}), bf16[16,64,1152]{2,1,0:T(8,128)(2,1)S(1)}, u32[]{:S(2)}, u32[]{:S(2)}) %all-to-all-start) | async-done | bytes 2359328 | tf_op jit(solution)/shard_map/all_to_all | solution.py:337
  48.1 1.8 %collective-permute-start = (bf16[16,64,1152]{2,1,0:T(8,128)(2,1)S(1)}, bf16[16,64,1152]{2,1,0:T(8,128)(2,1)S(1)}, u32[]{:S(2)}, u32[]{:S(2)}) collective-permute-start(bf16[16,64,1152]{2,1,0:T(8,128)(2,1)S(1)} %all-to-all-done.in_ref), channel_id=1, source_target_pairs={{0,32},{32,0},{1,33},{33,1},{2,34},{34,2},{3,35},{35,3},{4,36},{36... | collective-permute-start | bytes 7077896 | tf_op jit(solution)/shard_map/ppermute | solution.py:355
  49.9 0.8 arrange.1.mine_ref
  50.8 3.3 %collective-permute-done.partner_ref = bf16[16,64,1152]{2,1,0:T(8,128)(2,1)S(1)} collective-permute-done((bf16[16,64,1152]{2,1,0:T(8,128)(2,1)S(1)}, bf16[16,64,1152]{2,1,0:T(8,128)(2,1)S(1)}, u32[]{:S(2)}, u32[]{:S(2)}) %collective-permute-start) | collective-permute-done | bytes 2359328 | tf_op jit(solution)/shard_map/ppermute | solution.py:355
  54.1 0.0 copy-start
  54.1 22.6 %sketch.1 = bf16[4,2,4,16,512]{4,3,2,1,0:T(8,128)(2,1)} custom-call(s32[2]{0:T(128)S(1)} %pad_add_fusion.where_ref, s32[1152,128]{1,0:T(8,128)S(1)} %get-tuple-element.16.base_ref, bf16[16,2304,512]{2,1,0:T(8,128)(2,1)} %get-tuple-element.17.sign_hbm, bf16[8,64,2304]{2,1,0:T(8,128)(2,1)S(1)} %arrange.1.mine_ref, ...), custom_call_target="tpu_custom_call" | custom-call | tf_op jit(solution)/shard_map/sketch/pallas_call | solution.py:365
  76.7 4.2 %all-to-all-start.1 = ((bf16[32,16,512]{2,1,0:T(8,128)(2,1)}), bf16[32,16,512]{2,1,0:T(8,128)(2,1)S(1)}, u32[]{:S(2)}, u32[]{:S(2)}) async-start(bf16[32,16,512]{2,1,0:T(8,128)(2,1)} %bitcast.5), calls=%async_computation.1 | async-start | bytes 1048576 | tf_op jit(solution)/shard_map/all_to_all | solution.py:380
  80.9 11.4 %all-to-all-done.1.in_ref = bf16[32,16,512]{2,1,0:T(8,128)(2,1)S(1)} async-done(((bf16[32,16,512]{2,1,0:T(8,128)(2,1)}), bf16[32,16,512]{2,1,0:T(8,128)(2,1)S(1)}, u32[]{:S(2)}, u32[]{:S(2)}) %all-to-all-start.1) | async-done | bytes 524320 | tf_op jit(solution)/shard_map/all_to_all | solution.py:380
  92.3 0.0 copy-done
  92.3 0.8 route.1
  93.1 18.4 %all_to_all.15.in_ref = bf16[32,16,128]{2,1,0:T(8,128)(2,1)S(1)} all-to-all(bf16[32,16,128]{2,1,0:T(8,128)(2,1)S(1)} %route.1), channel_id=1, replica_groups=mesh['y'=4,'core'=2,'x'=4,'z'=8] {'x','z'}, dimensions={0} | all-to-all | bytes 262144 | tf_op jit(solution)/shard_map/all_to_all | solution.py:389
  111.6 0.6 finish.1
Async XLA Ops:
  5.8 7.6 %copy-start.1 = (s32[32]{0:T(128)S(1)}, s32[32]{0:T(128)}, u32[]{:S(2)}) copy-start(s32[32]{0:T(128)} %seeds_ref) | copy-start | bytes 388
  5.8 42.2 %all-to-all-start = ((bf16[16,64,1152]{2,1,0:T(8,128)(2,1)}), bf16[16,64,1152]{2,1,0:T(8,128)(2,1)S(1)}, u32[]{:S(2)}, u32[]{:S(2)}) async-start(bf16[16,64,1152]{2,1,0:T(8,128)(2,1)} %gradients.1), calls=%async_computation | async-start | bytes 4718592 | tf_op jit(solution)/shard_map/all_to_all | solution.py:337
  48.1 6.0 %collective-permute-start = (bf16[16,64,1152]{2,1,0:T(8,128)(2,1)S(1)}, bf16[16,64,1152]{2,1,0:T(8,128)(2,1)S(1)}, u32[]{:S(2)}, u32[]{:S(2)}) collective-permute-start(bf16[16,64,1152]{2,1,0:T(8,128)(2,1)S(1)} %all-to-all-done.in_ref), channel_id=1, source_target_pairs={{0,32},{32,0},{1,33},{33,1},{2,34},{34,2},{3,35},{35,3},{4,36},{36... | collective-permute-start | bytes 7077896 | tf_op jit(solution)/shard_map/ppermute | solution.py:355
  54.1 38.2 %copy-start = (s32[33]{0:T(128)S(1)}, s32[33]{0:T(128)}, u32[]{:S(2)}) copy-start(s32[33]{0:T(128)} %first_ref.1) | copy-start | bytes 400
  76.7 15.6 %all-to-all-start.1 = ((bf16[32,16,512]{2,1,0:T(8,128)(2,1)}), bf16[32,16,512]{2,1,0:T(8,128)(2,1)S(1)}, u32[]{:S(2)}, u32[]{:S(2)}) async-start(bf16[32,16,512]{2,1,0:T(8,128)(2,1)} %bitcast.5), calls=%async_computation.1 | async-start | bytes 1048576 | tf_op jit(solution)/shard_map/all_to_all | solution.py:380

commit v5 on v4

--- a/solution.py
+++ b/solution.py
@@ -31,7 +31,7 @@
 PIECES = NCORE * KTILE // LANES
 GROUPS = (3, 6, 9, 13, 16)
 DEPTH = 256
-EARLY = PAIRS // 2
+EARLY = 5
 
 
 def as_i32(value):
@@ -227,19 +227,22 @@
             for i in range(EARLY):
                 fetch((step + 1) * EARLY + i).start()
 
-        def pair(i, carry):
-            n = step * EARLY + i
-            slot = lax.rem(n, 2 * EARLY)
-            fetch(n).wait()
-            made = signs_of(base_ref, chip, EARLY + i, feature)
-            for q in range(0, 2 * COLS, DEPTH):
-                late = jnp.concatenate([next(made)[1] for _ in range(DEPTH // 16)], axis=0)
-                acc_ref[...] += jnp.dot(
-                    vectors(i, q), sign_ref[slot, q : q + DEPTH], preferred_element_type=F32
-                ) + jnp.dot(vectors(EARLY + i, q), late, preferred_element_type=F32)
-            return carry
-
-        lax.fori_loop(0, EARLY, pair, 0, unroll=True)
+        chunks = range(0, 2 * COLS, DEPTH)
+        stored = [(p, q) for p in range(EARLY) for q in chunks]
+        fresh = [(p, q) for p in range(EARLY, PAIRS) for q in chunks]
+        made = iter(())
+        for j, (p, q) in enumerate(fresh):
+            if q == 0:
+                made = signs_of(base_ref, chip, p, feature)
+            late = jnp.concatenate([next(made)[1] for _ in range(DEPTH // 16)], axis=0)
+            sums = jnp.dot(vectors(p, q), late, preferred_element_type=F32)
+            for e, at in stored[j * len(stored) // len(fresh) : (j + 1) * len(stored) // len(fresh)]:
+                n = step * EARLY + e
+                if at == 0:
+                    fetch(n).wait()
+                signs = sign_ref[lax.rem(n, 2 * EARLY), at : at + DEPTH].astype(BF16)
+                sums = sums + jnp.dot(vectors(e, at), signs, preferred_element_type=F32)
+            acc_ref[...] += sums
         total = acc_ref[...].astype(BF16)
         for half in range(NCORE):
             to_core = core if half == 0 else 1 - core
@@ -373,7 +376,7 @@
             pltpu.VMEM((2 * EARLY, 2 * COLS, KTILE), BF16),
             pltpu.SemaphoreType.DMA((2 * EARLY,)),
         ],
-        compiler_params=params(32),
+        compiler_params=params(40),
         name="sketch",
     )(where, base, in_hbm(early), mine, partner)
     parts = parts.reshape(NY * NCORE * NX, CUT_SLOTS, KTILE)

time: 112 us -> 109 us (0.973)
  waiting for transfers between devices: 28.6 us -> 23.8 us
  Pallas kernels: 51.3 us -> 52.7 us
    all_to_all x1, waiting for transfers between devices: 14 us -> 9.11 us  [body(): own = lax.all_to_all(grads, ('y', 'x'), 0, 0, tiled=True)]
    pallas_call x1, Pallas kernels: 20.7 us -> 25.5 us  [body(): pl.pallas_call(sign_kernel, out_shape=(pltpu.VMEM((COLS, LANES), I32), pl...]
    pallas_call x1, Pallas kernels: 22.6 us -> 19.1 us  [body(): pl.pallas_call(sketch_kernel, out_shape=jax.ShapeDtypeStruct((NY, NCORE,...]
  transfers between devices with their start and end apart: 3 -> 3, of which waited for: 3 -> 3; matrix products, arithmetic and copies ran while one was open for 0% -> 0% of each run, Pallas kernels for 19% -> 24%
where the time goes in v5:
time: 109 us
  Pallas kernels  52.7 us (48%)
  waiting for transfers between devices  23.8 us (22%)
  blocking collectives  18.4 us (17%)
  starting transfers between devices  13.7 us (13%)
    pallas_call x1, Pallas kernels, body(): pl.pallas_call(sign_kernel, out_shape=(pltpu.VMEM((COLS, LANES), I32), pl...  25.5 us
    pallas_call x1, Pallas kernels, body(): pl.pallas_call(sketch_kernel, out_shape=jax.ShapeDtypeStruct((NY, NCORE,...  19.1 us
    all_to_all x1, blocking collectives, body(): routed = lax.all_to_all(routed, ('x', 'z'), 0, 0, tiled=True)  18.4 us
    all_to_all x1, waiting for transfers between devices, body(): parts = lax.all_to_all(parts, ('y', 'core', 'x'), 0, 0, tiled=True)  11.4 us
    all_to_all x1, waiting for transfers between devices, body(): own = lax.all_to_all(grads, ('y', 'x'), 0, 0, tiled=True)  9.11 us
    all_to_all x1, starting transfers between devices, body(): own = lax.all_to_all(grads, ('y', 'x'), 0, 0, tiled=True)  7.59 us
    pallas_call x1, Pallas kernels, body(): pl.pallas_call(gradient_kernel, out_shape=pltpu.HBM((CHIPS, ROWS, COLS),...  5.77 us
    all_to_all x1, starting transfers between devices, body(): parts = lax.all_to_all(parts, ('y', 'core', 'x'), 0, 0, tiled=True)  4.24 us
  transfers between devices with their start and end apart: 3, of which 3 were waited for; matrix products, arithmetic and copies ran while one was open for 0% of the time, Pallas kernels for 24%

profile of v5, /device:TPU:1, one launch (start us, length us, event | category | flops | bytes accessed | tf_op | source)
XLA Modules:
  0.0 108.7 jit_solution(10317102653796797840)
XLA Ops:
  0.0 0.1 pad_add_fusion.where_ref
  0.1 5.8 %gradients.1 = bf16[16,64,1152]{2,1,0:T(8,128)(2,1)} custom-call(s32[1,128]{1,0:T(1,128)} %bitcast.7, s32[33]{0:T(128)} %first_ref.1, bf16[128,4096]{1,0:T(8,128)(2,1)} %act_hbm.1, bf16[128,14336]{1,0:T(8,128)(2,1)} %gout_hbm.1, bf16[16,4096]{1,0:T(8,128)(2,1)} %bitcast.6, bf16[16,14336]{1,0:T(8,128)(2,1)} %up_hbm.1), custom_call_target="tpu_custom_call" | custom-call | tf_op jit(solution)/shard_map/gradients/pallas_call | solution.py:319
  5.9 0.0 copy-start.1
  5.9 7.6 %all-to-all-start = ((bf16[16,64,1152]{2,1,0:T(8,128)(2,1)}), bf16[16,64,1152]{2,1,0:T(8,128)(2,1)S(1)}, u32[]{:S(2)}, u32[]{:S(2)}) async-start(bf16[16,64,1152]{2,1,0:T(8,128)(2,1)} %gradients.1), calls=%async_computation | async-start | bytes 4718592 | tf_op jit(solution)/shard_map/all_to_all | solution.py:340
  13.5 0.0 copy-done.1
  13.5 25.5 %signs.1 = (s32[1152,128]{1,0:T(8,128)S(1)}, bf16[20,2304,512]{2,1,0:T(8,128)(2,1)}) custom-call(s32[2]{0:T(128)S(1)} %pad_add_fusion.where_ref, s32[32]{0:T(128)S(1)} %copy-done.1), custom_call_target="tpu_custom_call" | custom-call | flops 20000000000 | tf_op jit(solution)/shard_map/signs/pallas_call | solution.py:341
  39.0 9.1 %all-to-all-done.in_ref = bf16[16,64,1152]{2,1,0:T(8,128)(2,1)S(1)} async-done(((bf16[16,64,1152]{2,1,0:T(8,128)(2,1)}), bf16[16,64,1152]{2,1,0:T(8,128)(2,1)S(1)}, u32[]{:S(2)}, u32[]{:S(2)}) %all-to-all-start) | async-done | bytes 2359328 | tf_op jit(solution)/shard_map/all_to_all | solution.py:340
  48.1 1.8 %collective-permute-start = (bf16[16,64,1152]{2,1,0:T(8,128)(2,1)S(1)}, bf16[16,64,1152]{2,1,0:T(8,128)(2,1)S(1)}, u32[]{:S(2)}, u32[]{:S(2)}) collective-permute-start(bf16[16,64,1152]{2,1,0:T(8,128)(2,1)S(1)} %all-to-all-done.in_ref), channel_id=1, source_target_pairs={{0,32},{32,0},{1,33},{33,1},{2,34},{34,2},{3,35},{35,3},{4,36},{36... | collective-permute-start | bytes 7077896 | tf_op jit(solution)/shard_map/ppermute | solution.py:358
  49.9 0.8 arrange.1.mine_ref
  50.8 3.3 %collective-permute-done.partner_ref = bf16[16,64,1152]{2,1,0:T(8,128)(2,1)S(1)} collective-permute-done((bf16[16,64,1152]{2,1,0:T(8,128)(2,1)S(1)}, bf16[16,64,1152]{2,1,0:T(8,128)(2,1)S(1)}, u32[]{:S(2)}, u32[]{:S(2)}) %collective-permute-start) | collective-permute-done | bytes 2359328 | tf_op jit(solution)/shard_map/ppermute | solution.py:358
  54.1 0.0 copy-start
  54.1 19.1 %sketch.1 = bf16[4,2,4,16,512]{4,3,2,1,0:T(8,128)(2,1)} custom-call(s32[2]{0:T(128)S(1)} %pad_add_fusion.where_ref, s32[1152,128]{1,0:T(8,128)S(1)} %get-tuple-element.16.base_ref, bf16[20,2304,512]{2,1,0:T(8,128)(2,1)} %get-tuple-element.17.sign_hbm, bf16[8,64,2304]{2,1,0:T(8,128)(2,1)S(1)} %arrange.1.mine_ref, ...), custom_call_target="tpu_custom_call" | custom-call | tf_op jit(solution)/shard_map/sketch/pallas_call | solution.py:368
  73.2 4.2 %all-to-all-start.1 = ((bf16[32,16,512]{2,1,0:T(8,128)(2,1)}), bf16[32,16,512]{2,1,0:T(8,128)(2,1)S(1)}, u32[]{:S(2)}, u32[]{:S(2)}) async-start(bf16[32,16,512]{2,1,0:T(8,128)(2,1)} %bitcast.5), calls=%async_computation.1 | async-start | bytes 1048576 | tf_op jit(solution)/shard_map/all_to_all | solution.py:383
  77.5 11.4 %all-to-all-done.1.in_ref = bf16[32,16,512]{2,1,0:T(8,128)(2,1)S(1)} async-done(((bf16[32,16,512]{2,1,0:T(8,128)(2,1)}), bf16[32,16,512]{2,1,0:T(8,128)(2,1)S(1)}, u32[]{:S(2)}, u32[]{:S(2)}) %all-to-all-start.1) | async-done | bytes 524320 | tf_op jit(solution)/shard_map/all_to_all | solution.py:383
  88.8 0.0 copy-done
  88.8 0.8 route.1
  89.6 18.4 %all_to_all.15.in_ref = bf16[32,16,128]{2,1,0:T(8,128)(2,1)S(1)} all-to-all(bf16[32,16,128]{2,1,0:T(8,128)(2,1)S(1)} %route.1), channel_id=1, replica_groups=mesh['y'=4,'core'=2,'x'=4,'z'=8] {'x','z'}, dimensions={0} | all-to-all | bytes 262144 | tf_op jit(solution)/shard_map/all_to_all | solution.py:392
  108.1 0.6 finish.1
Async XLA Ops:
  5.9 7.6 %copy-start.1 = (s32[32]{0:T(128)S(1)}, s32[32]{0:T(128)}, u32[]{:S(2)}) copy-start(s32[32]{0:T(128)} %seeds_ref) | copy-start | bytes 388
  5.9 42.2 %all-to-all-start = ((bf16[16,64,1152]{2,1,0:T(8,128)(2,1)}), bf16[16,64,1152]{2,1,0:T(8,128)(2,1)S(1)}, u32[]{:S(2)}, u32[]{:S(2)}) async-start(bf16[16,64,1152]{2,1,0:T(8,128)(2,1)} %gradients.1), calls=%async_computation | async-start | bytes 4718592 | tf_op jit(solution)/shard_map/all_to_all | solution.py:340
  48.1 6.0 %collective-permute-start = (bf16[16,64,1152]{2,1,0:T(8,128)(2,1)S(1)}, bf16[16,64,1152]{2,1,0:T(8,128)(2,1)S(1)}, u32[]{:S(2)}, u32[]{:S(2)}) collective-permute-start(bf16[16,64,1152]{2,1,0:T(8,128)(2,1)S(1)} %all-to-all-done.in_ref), channel_id=1, source_target_pairs={{0,32},{32,0},{1,33},{33,1},{2,34},{34,2},{3,35},{35,3},{4,36},{36... | collective-permute-start | bytes 7077896 | tf_op jit(solution)/shard_map/ppermute | solution.py:358
  54.1 34.8 %copy-start = (s32[33]{0:T(128)S(1)}, s32[33]{0:T(128)}, u32[]{:S(2)}) copy-start(s32[33]{0:T(128)} %first_ref.1) | copy-start | bytes 400
  73.2 15.6 %all-to-all-start.1 = ((bf16[32,16,512]{2,1,0:T(8,128)(2,1)}), bf16[32,16,512]{2,1,0:T(8,128)(2,1)S(1)}, u32[]{:S(2)}, u32[]{:S(2)}) async-start(bf16[32,16,512]{2,1,0:T(8,128)(2,1)} %bitcast.5), calls=%async_computation.1 | async-start | bytes 1048576 | tf_op jit(solution)/shard_map/all_to_all | solution.py:383

commit v6 on v5

--- a/solution.py
+++ b/solution.py
@@ -31,7 +31,7 @@
 PIECES = NCORE * KTILE // LANES
 GROUPS = (3, 6, 9, 13, 16)
 DEPTH = 256
-EARLY = 5
+EARLY = 7
 
 
 def as_i32(value):
@@ -46,6 +46,7 @@
 F32 = jnp.float32
 BF16 = jnp.bfloat16
 I32 = jnp.int32
+F8 = jnp.float8_e4m3fn
 
 
 def iota(shape, dim):
@@ -172,8 +173,12 @@
 
         slot = lax.rem(i, 2)
         tile, p = i // EARLY, lax.rem(i, EARLY)
+        upper = None
         for row, signs in signs_of(base_ref, chip, p, first_feature(core, tile)):
-            made_ref[slot, row : row + 16] = signs
+            if row % 32:
+                both = jnp.concatenate([upper, signs], axis=0)
+                made_ref[slot, row - 16 : row + 16] = both.astype(F8)
+            upper = signs
         send(i).start()
         return carry
 
@@ -209,9 +214,11 @@
         slot = lax.rem(i, 2 * EARLY)
         return pltpu.make_async_copy(sign_hbm.at[i], sign_ref.at[slot], sems.at[slot])
 
-    for i in range(EARLY):
+    for i in range(2):
         fetch(i).start()
     arrange(partner_ref, vec_ref)
+    for i in range(2, EARLY):
+        fetch(i).start()
 
     def vectors(p, q):
         return jnp.concatenate(
@@ -254,7 +261,9 @@
     lax.fori_loop(0, NX, tile, 0)
 
 
-def route_kernel(first_ref, z_ref, in_ref, out_ref):
+def route_kernel(first_hbm, in_ref, out_ref, first_ref, sem):
+    copy = pltpu.make_async_copy(first_hbm, first_ref, sem)
+    copy.start()
     sums = []
     for c in range(NCORE):
         total = jnp.zeros((CUT_SLOTS, KTILE), F32)
@@ -270,7 +279,8 @@
         ],
         axis=0,
     )
-    z = z_ref[0]
+    z = lax.axis_index("z")
+    copy.wait()
     width = PIECES * CUT_SLOTS
     row, col = iota((EXAMPLES * PIECES, width), 0), iota((EXAMPLES * PIECES, width), 1)
     slot = lax.rem(col, CUT_SLOTS)
@@ -315,7 +325,7 @@
 
 
 def body(acts, gouts, adapter_down, adapter_up, token_example, cut_first, seeds):
-    y, core, x, z = (lax.axis_index(name) for name in ("y", "core", "x", "z"))
+    y, core, x = (lax.axis_index(name) for name in ("y", "core", "x"))
     grads = pl.pallas_call(
         gradient_kernel,
         out_shape=pltpu.HBM((CHIPS, ROWS, COLS), BF16),
@@ -342,12 +352,12 @@
         sign_kernel,
         out_shape=(
             pltpu.VMEM((COLS, LANES), I32),
-            pltpu.HBM((NX * EARLY, 2 * COLS, KTILE), BF16),
+            pltpu.HBM((NX * EARLY, 2 * COLS, KTILE), F8),
         ),
         in_specs=[SMEM, SMEM],
         out_specs=(VMEM, HBM),
         scratch_shapes=[
-            pltpu.VMEM((2, 2 * COLS, KTILE), BF16),
+            pltpu.VMEM((2, 2 * COLS, KTILE), F8),
             pltpu.SemaphoreType.DMA((2,)),
         ],
         cost_estimate=pl.CostEstimate(flops=20_000_000_000, bytes_accessed=0, transcendentals=0),
@@ -373,7 +383,7 @@
         scratch_shapes=[
             pltpu.VMEM((PAIRS, SLOTS // NCORE, 2 * COLS), BF16),
             pltpu.VMEM((SLOTS, KTILE), F32),
-            pltpu.VMEM((2 * EARLY, 2 * COLS, KTILE), BF16),
+            pltpu.VMEM((2 * EARLY, 2 * COLS, KTILE), F8),
             pltpu.SemaphoreType.DMA((2 * EARLY,)),
         ],
         compiler_params=params(40),
@@ -384,11 +394,12 @@
     routed = pl.pallas_call(
         route_kernel,
         out_shape=jax.ShapeDtypeStruct((NX * NZ, 2 * PIECES, LANES), BF16),
-        in_specs=[SMEM, SMEM, VMEM],
+        in_specs=[HBM, VMEM],
         out_specs=VMEM,
+        scratch_shapes=[pltpu.SMEM((cut_first.shape[0],), I32), pltpu.SemaphoreType.DMA],
         compiler_params=params(32),
         name="route",
-    )(cut_first, z.astype(I32).reshape(1), parts)
+    )(in_hbm(cut_first), parts)
     routed = lax.all_to_all(routed, ("x", "z"), 0, 0, tiled=True)
     return pl.pallas_call(
         finish_kernel,

time: 109 us -> 105 us (0.963)
  blocking collectives: 18.4 us -> 33.8 us
  waiting for transfers between devices: 23.8 us -> 9.03 us
  starting transfers between devices: 13.7 us -> 9.42 us
    all_to_all x0 -> x1, blocking collectives: none -> 15.4 us  [body(): parts = lax.all_to_all(parts, ('y', 'core', 'x'), 0, 0, tiled=True)]
    all_to_all x1 -> x0, waiting for transfers between devices: 11.4 us -> none  [body(): parts = lax.all_to_all(parts, ('y', 'core', 'x'), 0, 0, tiled=True)]
    all_to_all x1 -> x0, starting transfers between devices: 4.24 us -> none  [body(): parts = lax.all_to_all(parts, ('y', 'core', 'x'), 0, 0, tiled=True)]
    all_to_all x1, waiting for transfers between devices: 9.11 us -> 5.72 us  [body(): own = lax.all_to_all(grads, ('y', 'x'), 0, 0, tiled=True)]
    pallas_call x1, Pallas kernels: 25.5 us -> 28.9 us  [body(): pl.pallas_call(sign_kernel, out_shape=(pltpu.VMEM((COLS, LANES), I32), pl...]
    pallas_call x1, Pallas kernels: 19.1 us -> 15.7 us  [body(): pl.pallas_call(sketch_kernel, out_shape=jax.ShapeDtypeStruct((NY, NCORE,...]
  transfers between devices with their start and end apart: 3 -> 2, of which waited for: 3 -> 2; matrix products, arithmetic and copies ran while one was open for 0% -> 0% of each run, Pallas kernels for 24% -> 28%
where the time goes in v6:
time: 105 us
  Pallas kernels  52.7 us (50%)
  blocking collectives  33.8 us (32%)
  starting transfers between devices  9.42 us (9%)
  waiting for transfers between devices  9.03 us (9%)
    pallas_call x1, Pallas kernels, body(): pl.pallas_call(sign_kernel, out_shape=(pltpu.VMEM((COLS, LANES), I32), pl...  28.9 us
    all_to_all x1, blocking collectives, body(): routed = lax.all_to_all(routed, ('x', 'z'), 0, 0, tiled=True)  18.4 us
    pallas_call x1, Pallas kernels, body(): pl.pallas_call(sketch_kernel, out_shape=jax.ShapeDtypeStruct((NY, NCORE,...  15.7 us
    all_to_all x1, blocking collectives, body(): parts = lax.all_to_all(parts, ('y', 'core', 'x'), 0, 0, tiled=True)  15.4 us
    all_to_all x1, starting transfers between devices, body(): own = lax.all_to_all(grads, ('y', 'x'), 0, 0, tiled=True)  7.59 us
    pallas_call x1, Pallas kernels, body(): pl.pallas_call(gradient_kernel, out_shape=pltpu.HBM((CHIPS, ROWS, COLS),...  5.76 us
    all_to_all x1, waiting for transfers between devices, body(): own = lax.all_to_all(grads, ('y', 'x'), 0, 0, tiled=True)  5.72 us
    ppermute x1, waiting for transfers between devices, body(): partner = lax.ppermute(own, 'core', [(0, 1), (1, 0)])  3.31 us
  transfers between devices with their start and end apart: 2, of which 2 were waited for; matrix products, arithmetic and copies ran while one was open for 0% of the time, Pallas kernels for 28%

profile of v6, /device:TPU:1, one launch (start us, length us, event | category | flops | bytes accessed | tf_op | source)
XLA Modules:
  0.0 105.2 jit_solution(16657225039767416647)
XLA Ops:
  0.0 0.1 pad_add_fusion.where_ref
  0.1 5.8 %gradients.1 = bf16[16,64,1152]{2,1,0:T(8,128)(2,1)} custom-call(s32[1,128]{1,0:T(1,128)} %bitcast.7, s32[33]{0:T(128)} %first_hbm.3, bf16[128,4096]{1,0:T(8,128)(2,1)} %act_hbm.1, bf16[128,14336]{1,0:T(8,128)(2,1)} %gout_hbm.1, bf16[16,4096]{1,0:T(8,128)(2,1)} %bitcast.6, bf16[16,14336]{1,0:T(8,128)(2,1)} %up_hbm.1), custom_call_target="tpu_custom_call" | custom-call | tf_op jit(solution)/shard_map/gradients/pallas_call | solution.py:329
  5.8 0.0 copy-start
  5.9 7.6 %all-to-all-start = ((bf16[16,64,1152]{2,1,0:T(8,128)(2,1)}), bf16[16,64,1152]{2,1,0:T(8,128)(2,1)S(1)}, u32[]{:S(2)}, u32[]{:S(2)}) async-start(bf16[16,64,1152]{2,1,0:T(8,128)(2,1)} %gradients.1), calls=%async_computation | async-start | bytes 4718592 | tf_op jit(solution)/shard_map/all_to_all | solution.py:350
  13.5 0.0 copy-done
  13.5 28.9 %signs.1 = (s32[1152,128]{1,0:T(8,128)S(1)}, f8e4m3fn[28,2304,512]{2,1,0:T(32,128)(4,1)}) custom-call(s32[2]{0:T(128)S(1)} %pad_add_fusion.where_ref, s32[32]{0:T(128)S(1)} %copy-done), custom_call_target="tpu_custom_call" | custom-call | flops 20000000000 | tf_op jit(solution)/shard_map/signs/pallas_call | solution.py:351
  42.3 5.7 %all-to-all-done.in_ref = bf16[16,64,1152]{2,1,0:T(8,128)(2,1)S(1)} async-done(((bf16[16,64,1152]{2,1,0:T(8,128)(2,1)}), bf16[16,64,1152]{2,1,0:T(8,128)(2,1)S(1)}, u32[]{:S(2)}, u32[]{:S(2)}) %all-to-all-start) | async-done | bytes 2359328 | tf_op jit(solution)/shard_map/all_to_all | solution.py:350
  48.1 1.8 %collective-permute-start = (bf16[16,64,1152]{2,1,0:T(8,128)(2,1)S(1)}, bf16[16,64,1152]{2,1,0:T(8,128)(2,1)S(1)}, u32[]{:S(2)}, u32[]{:S(2)}) collective-permute-start(bf16[16,64,1152]{2,1,0:T(8,128)(2,1)S(1)} %all-to-all-done.in_ref), channel_id=1, source_target_pairs={{0,32},{32,0},{1,33},{33,1},{2,34},{34,2},{3,35},{35,3},{4,36},{36... | collective-permute-start | bytes 7077896 | tf_op jit(solution)/shard_map/ppermute | solution.py:368
  49.9 0.8 arrange.1.mine_ref
  50.8 3.3 %collective-permute-done.partner_ref = bf16[16,64,1152]{2,1,0:T(8,128)(2,1)S(1)} collective-permute-done((bf16[16,64,1152]{2,1,0:T(8,128)(2,1)S(1)}, bf16[16,64,1152]{2,1,0:T(8,128)(2,1)S(1)}, u32[]{:S(2)}, u32[]{:S(2)}) %collective-permute-start) | collective-permute-done | bytes 2359328 | tf_op jit(solution)/shard_map/ppermute | solution.py:368
  54.1 15.7 %sketch.1 = bf16[4,2,4,16,512]{4,3,2,1,0:T(8,128)(2,1)S(1)} custom-call(s32[2]{0:T(128)S(1)} %pad_add_fusion.where_ref, s32[1152,128]{1,0:T(8,128)S(1)} %get-tuple-element.16.base_ref, f8e4m3fn[28,2304,512]{2,1,0:T(32,128)(4,1)} %get-tuple-element.17.sign_hbm, bf16[8,64,2304]{2,1,0:T(8,128)(2,1)S(1)} %arrange.1.mine_ref, ...), custom_call_target="tpu_custom_call" | custom-call | tf_op jit(solution)/shard_map/sketch/pallas_call | solution.py:378
  69.8 15.4 %all_to_all.15.in_ref = bf16[32,16,512]{2,1,0:T(8,128)(2,1)S(1)} all-to-all(bf16[32,16,512]{2,1,0:T(8,128)(2,1)S(1)} %bitcast.5), channel_id=1, replica_groups=mesh['y'=4,'core'=2,'x'=4,'z'=8] {'y','core','x'}, dimensions={0} | all-to-all | bytes 1048576 | tf_op jit(solution)/shard_map/all_to_all | solution.py:393
  85.2 0.9 route.1
  86.1 18.4 %all_to_all.16.in_ref = bf16[32,16,128]{2,1,0:T(8,128)(2,1)S(1)} all-to-all(bf16[32,16,128]{2,1,0:T(8,128)(2,1)S(1)} %route.1), channel_id=1, replica_groups=mesh['y'=4,'core'=2,'x'=4,'z'=8] {'x','z'}, dimensions={0} | all-to-all | bytes 262144 | tf_op jit(solution)/shard_map/all_to_all | solution.py:403
  104.5 0.6 finish.1
Async XLA Ops:
  5.8 7.6 %copy-start = (s32[32]{0:T(128)S(1)}, s32[32]{0:T(128)}, u32[]{:S(2)}) copy-start(s32[32]{0:T(128)} %seeds_ref) | copy-start | bytes 388
  5.9 42.2 %all-to-all-start = ((bf16[16,64,1152]{2,1,0:T(8,128)(2,1)}), bf16[16,64,1152]{2,1,0:T(8,128)(2,1)S(1)}, u32[]{:S(2)}, u32[]{:S(2)}) async-start(bf16[16,64,1152]{2,1,0:T(8,128)(2,1)} %gradients.1), calls=%async_computation | async-start | bytes 4718592 | tf_op jit(solution)/shard_map/all_to_all | solution.py:350
  48.1 6.0 %collective-permute-start = (bf16[16,64,1152]{2,1,0:T(8,128)(2,1)S(1)}, bf16[16,64,1152]{2,1,0:T(8,128)(2,1)S(1)}, u32[]{:S(2)}, u32[]{:S(2)}) collective-permute-start(bf16[16,64,1152]{2,1,0:T(8,128)(2,1)S(1)} %all-to-all-done.in_ref), channel_id=1, source_target_pairs={{0,32},{32,0},{1,33},{33,1},{2,34},{34,2},{3,35},{35,3},{4,36},{36... | collective-permute-start | bytes 7077896 | tf_op jit(solution)/shard_map/ppermute | solution.py:368

commit v7 on v6

--- a/solution.py
+++ b/solution.py
@@ -247,7 +247,7 @@
                 n = step * EARLY + e
                 if at == 0:
                     fetch(n).wait()
-                signs = sign_ref[lax.rem(n, 2 * EARLY), at : at + DEPTH].astype(BF16)
+                signs = sign_ref[lax.rem(n, 2 * EARLY), at : at + DEPTH]
                 sums = sums + jnp.dot(vectors(e, at), signs, preferred_element_type=F32)
             acc_ref[...] += sums
         total = acc_ref[...].astype(BF16)

time: 105 us -> 104 us (level)
  Pallas kernels: 52.7 us -> 51.5 us
    pallas_call x1, Pallas kernels: 15.7 us -> 14.5 us  [body(): pl.pallas_call(sketch_kernel, out_shape=jax.ShapeDtypeStruct((NY, NCORE,...]
  transfers between devices with their start and end apart: 2 -> 2, of which waited for: 2 -> 2; matrix products, arithmetic and copies ran while one was open for 0% -> 0% of each run, Pallas kernels for 28% -> 29%
where the time goes in v7:
time: 104 us
  Pallas kernels  51.5 us (50%)
  blocking collectives  33.8 us (32%)
  starting transfers between devices  9.42 us (9%)
  waiting for transfers between devices  9.03 us (9%)
    pallas_call x1, Pallas kernels, body(): pl.pallas_call(sign_kernel, out_shape=(pltpu.VMEM((COLS, LANES), I32), pl...  28.9 us
    all_to_all x1, blocking collectives, body(): routed = lax.all_to_all(routed, ('x', 'z'), 0, 0, tiled=True)  18.4 us
    all_to_all x1, blocking collectives, body(): parts = lax.all_to_all(parts, ('y', 'core', 'x'), 0, 0, tiled=True)  15.4 us
    pallas_call x1, Pallas kernels, body(): pl.pallas_call(sketch_kernel, out_shape=jax.ShapeDtypeStruct((NY, NCORE,...  14.5 us
    all_to_all x1, starting transfers between devices, body(): own = lax.all_to_all(grads, ('y', 'x'), 0, 0, tiled=True)  7.59 us
    pallas_call x1, Pallas kernels, body(): pl.pallas_call(gradient_kernel, out_shape=pltpu.HBM((CHIPS, ROWS, COLS),...  5.76 us
    all_to_all x1, waiting for transfers between devices, body(): own = lax.all_to_all(grads, ('y', 'x'), 0, 0, tiled=True)  5.72 us
    ppermute x1, waiting for transfers between devices, body(): partner = lax.ppermute(own, 'core', [(0, 1), (1, 0)])  3.31 us
  transfers between devices with their start and end apart: 2, of which 2 were waited for; matrix products, arithmetic and copies ran while one was open for 0% of the time, Pallas kernels for 29%

profile of v7, /device:TPU:1, one launch (start us, length us, event | category | flops | bytes accessed | tf_op | source)
XLA Modules:
  0.0 103.9 jit_solution(1247632589855846602)
XLA Ops:
  0.0 0.1 pad_add_fusion.where_ref
  0.1 5.8 %gradients.1 = bf16[16,64,1152]{2,1,0:T(8,128)(2,1)} custom-call(s32[1,128]{1,0:T(1,128)} %bitcast.7, s32[33]{0:T(128)} %first_hbm.3, bf16[128,4096]{1,0:T(8,128)(2,1)} %act_hbm.1, bf16[128,14336]{1,0:T(8,128)(2,1)} %gout_hbm.1, bf16[16,4096]{1,0:T(8,128)(2,1)} %bitcast.6, bf16[16,14336]{1,0:T(8,128)(2,1)} %up_hbm.1), custom_call_target="tpu_custom_call" | custom-call | tf_op jit(solution)/shard_map/gradients/pallas_call | solution.py:329
  5.8 0.0 copy-start
  5.9 7.6 %all-to-all-start = ((bf16[16,64,1152]{2,1,0:T(8,128)(2,1)}), bf16[16,64,1152]{2,1,0:T(8,128)(2,1)S(1)}, u32[]{:S(2)}, u32[]{:S(2)}) async-start(bf16[16,64,1152]{2,1,0:T(8,128)(2,1)} %gradients.1), calls=%async_computation | async-start | bytes 4718592 | tf_op jit(solution)/shard_map/all_to_all | solution.py:350
  13.5 0.0 copy-done
  13.5 28.9 %signs.1 = (s32[1152,128]{1,0:T(8,128)S(1)}, f8e4m3fn[28,2304,512]{2,1,0:T(32,128)(4,1)}) custom-call(s32[2]{0:T(128)S(1)} %pad_add_fusion.where_ref, s32[32]{0:T(128)S(1)} %copy-done), custom_call_target="tpu_custom_call" | custom-call | flops 20000000000 | tf_op jit(solution)/shard_map/signs/pallas_call | solution.py:351
  42.3 5.7 %all-to-all-done.in_ref = bf16[16,64,1152]{2,1,0:T(8,128)(2,1)S(1)} async-done(((bf16[16,64,1152]{2,1,0:T(8,128)(2,1)}), bf16[16,64,1152]{2,1,0:T(8,128)(2,1)S(1)}, u32[]{:S(2)}, u32[]{:S(2)}) %all-to-all-start) | async-done | bytes 2359328 | tf_op jit(solution)/shard_map/all_to_all | solution.py:350
  48.1 1.8 %collective-permute-start = (bf16[16,64,1152]{2,1,0:T(8,128)(2,1)S(1)}, bf16[16,64,1152]{2,1,0:T(8,128)(2,1)S(1)}, u32[]{:S(2)}, u32[]{:S(2)}) collective-permute-start(bf16[16,64,1152]{2,1,0:T(8,128)(2,1)S(1)} %all-to-all-done.in_ref), channel_id=1, source_target_pairs={{0,32},{32,0},{1,33},{33,1},{2,34},{34,2},{3,35},{35,3},{4,36},{36... | collective-permute-start | bytes 7077896 | tf_op jit(solution)/shard_map/ppermute | solution.py:368
  49.9 0.8 arrange.1.mine_ref
  50.8 3.3 %collective-permute-done.partner_ref = bf16[16,64,1152]{2,1,0:T(8,128)(2,1)S(1)} collective-permute-done((bf16[16,64,1152]{2,1,0:T(8,128)(2,1)S(1)}, bf16[16,64,1152]{2,1,0:T(8,128)(2,1)S(1)}, u32[]{:S(2)}, u32[]{:S(2)}) %collective-permute-start) | collective-permute-done | bytes 2359328 | tf_op jit(solution)/shard_map/ppermute | solution.py:368
  54.1 14.5 %sketch.1 = bf16[4,2,4,16,512]{4,3,2,1,0:T(8,128)(2,1)S(1)} custom-call(s32[2]{0:T(128)S(1)} %pad_add_fusion.where_ref, s32[1152,128]{1,0:T(8,128)S(1)} %get-tuple-element.16.base_ref, f8e4m3fn[28,2304,512]{2,1,0:T(32,128)(4,1)} %get-tuple-element.17.sign_hbm, bf16[8,64,2304]{2,1,0:T(8,128)(2,1)S(1)} %arrange.1.mine_ref, ...), custom_call_target="tpu_custom_call" | custom-call | tf_op jit(solution)/shard_map/sketch/pallas_call | solution.py:378
  68.5 15.4 %all_to_all.15.in_ref = bf16[32,16,512]{2,1,0:T(8,128)(2,1)S(1)} all-to-all(bf16[32,16,512]{2,1,0:T(8,128)(2,1)S(1)} %bitcast.5), channel_id=1, replica_groups=mesh['y'=4,'core'=2,'x'=4,'z'=8] {'y','core','x'}, dimensions={0} | all-to-all | bytes 1048576 | tf_op jit(solution)/shard_map/all_to_all | solution.py:393
  83.9 0.9 route.1
  84.8 18.4 %all_to_all.16.in_ref = bf16[32,16,128]{2,1,0:T(8,128)(2,1)S(1)} all-to-all(bf16[32,16,128]{2,1,0:T(8,128)(2,1)S(1)} %route.1), channel_id=1, replica_groups=mesh['y'=4,'core'=2,'x'=4,'z'=8] {'x','z'}, dimensions={0} | all-to-all | bytes 262144 | tf_op jit(solution)/shard_map/all_to_all | solution.py:403
  103.2 0.6 finish.1
Async XLA Ops:
  5.8 7.6 %copy-start = (s32[32]{0:T(128)S(1)}, s32[32]{0:T(128)}, u32[]{:S(2)}) copy-start(s32[32]{0:T(128)} %seeds_ref) | copy-start | bytes 388
  5.9 42.2 %all-to-all-start = ((bf16[16,64,1152]{2,1,0:T(8,128)(2,1)}), bf16[16,64,1152]{2,1,0:T(8,128)(2,1)S(1)}, u32[]{:S(2)}, u32[]{:S(2)}) async-start(bf16[16,64,1152]{2,1,0:T(8,128)(2,1)} %gradients.1), calls=%async_computation | async-start | bytes 4718592 | tf_op jit(solution)/shard_map/all_to_all | solution.py:350
  48.1 6.0 %collective-permute-start = (bf16[16,64,1152]{2,1,0:T(8,128)(2,1)S(1)}, bf16[16,64,1152]{2,1,0:T(8,128)(2,1)S(1)}, u32[]{:S(2)}, u32[]{:S(2)}) collective-permute-start(bf16[16,64,1152]{2,1,0:T(8,128)(2,1)S(1)} %all-to-all-done.in_ref), channel_id=1, source_target_pairs={{0,32},{32,0},{1,33},{33,1},{2,34},{34,2},{3,35},{35,3},{4,36},{36... | collective-permute-start | bytes 7077896 | tf_op jit(solution)/shard_map/ppermute | solution.py:368
